TPU v7x, 512 devices: a whole 4x4x16 slice. The times are simulated.
512 devices in a mesh: head: 8 (over x, core), ctx: 64 (over y, z).
Axes of the slice: x: 4, y: 4, z: 16, core: 2. Of those that a mesh axis runs over, the one named last changes fastest.
Arguments:
- queries: bfloat16 [65536, 4096], P('ctx', 'head'), may hold values from -24 to 24
- keys: bfloat16 [65536, 1024], P('ctx', 'head'), may hold values from -24 to 24
- values: bfloat16 [65536, 1024], P('ctx', 'head'), may hold values from -6 to 6
- vertical_ids: int32 [8, 8], P('head'), may hold values from 0 to 511, as said below
- slash_offsets: int32 [8, 2], P('head'), may hold values from 1 to 8, as said below
- keep_counts: int32 [8, 512], P('head', 'ctx'), may hold values from 1 to 8
Outputs:
- attended: bfloat16 [65536, 4096], P('ctx', 'head')
- column_scores: float32 [65536], P('ctx')
- vertical_scores: float32 [8, 8, 128], P('head')
Inputs may be any that keep to these rules, and one draw needn't show every extreme that they name: `vertical_ids`: the entries of a row are distinct and the first is 0. `slash_offsets`: the entries of a row are distinct and the first is 8.
All inputs are finite; a program needn't handle non-finite values.
Results may differ from a plain program's by a relative error of at most 0.0049.
Values may be sent and summed in bfloat16 or wider, within the bound.
A program may use at most 64 MiB of HBM per device.

v0:
```python
import jax
import jax.numpy as jnp
from jax import lax
from jax.sharding import PartitionSpec as P

QPK = 4
TILE = 128


def shifted(block, axis, distance):
    devices = range(lax.axis_size(axis))
    route = [(i - distance, i) for i in devices if i - distance in devices]
    return lax.ppermute(block, axis, route)


def spread(value, axis, source):
    kept = jnp.where(lax.axis_index(axis) == source, value, 0).astype(value.dtype)
    return lax.psum(kept, axis)


def tile_slices(source, starts, width):
    return jax.vmap(lambda start: lax.dynamic_slice_in_dim(source, start, width, 1))(starts)


def local(queries, keys, values, vertical_ids, slash_offsets, keep_counts):
    tok_rows, head_dim = keys.shape
    tile_count = tok_rows // TILE
    first_tile = lax.axis_index("ctx") * tile_count
    key_value = jnp.stack([keys, values])
    before = shifted(key_value, "ctx", 1)
    window_rows = jnp.concatenate([before, key_value], axis=1)
    vertical = vertical_ids[0]
    vertical_count = vertical.shape[0]

    def fetch_tile(slot, gathered):
        tile_id = vertical[slot]
        piece = lax.dynamic_slice_in_dim(key_value, tile_id % tile_count * TILE, TILE, 1)
        arrived = spread(piece, "ctx", tile_id // tile_count)
        return lax.dynamic_update_index_in_dim(gathered, arrived, slot, 0)

    fetched = lax.fori_loop(
        0, vertical_count, fetch_tile, jnp.zeros((vertical_count, 2, TILE, head_dim), jnp.bfloat16)
    )
    slash = slash_offsets[0]
    slash_count = slash.shape[0]
    keep_list = keep_counts[0]
    query_tiles = queries.reshape(tile_count, TILE * QPK, head_dim)
    slot_total = 1 + slash_count + vertical_count
    positions = jnp.arange(TILE)
    row_position = jnp.repeat(positions, QPK)
    causal = row_position[:, None] >= positions[None, :]
    not_diagonal = jnp.arange(slot_total) != 0
    window_count = 2 * tile_count
    scale = head_dim ** (-0.5)

    def per_tile(carry, tile_index):
        window_sums, vertical_sums = carry
        global_tile = first_tile + tile_index
        slash_ids = global_tile - slash
        slash_valid = slash_ids >= 0
        repeated = jnp.any(
            (vertical[:, None] == slash_ids[None, :]) & slash_valid[None, :], axis=1
        ) | (vertical == global_tile)
        vertical_valid = (
            (jnp.arange(vertical_count) < keep_list[tile_index])
            & (vertical <= global_tile)
            & jnp.logical_not(repeated)
        )
        valid = jnp.concatenate([jnp.ones((1,), bool), slash_valid, vertical_valid])
        window_index = jnp.concatenate(
            [(tile_count + tile_index)[None], tile_count + tile_index - slash]
        )
        nearby = tile_slices(window_rows, window_index * TILE, TILE)
        chosen = jnp.concatenate([nearby, fetched], axis=0)
        key_rows = chosen[:, 0].reshape(slot_total * TILE, head_dim)
        value_rows = chosen[:, 1].reshape(slot_total * TILE, head_dim)
        query_rows = lax.dynamic_index_in_dim(query_tiles, tile_index, 0, keepdims=False)
        scores = (
            lax.dot_general(
                query_rows, key_rows, (((1,), (1,)), ((), ())), preferred_element_type=jnp.float32
            )
            * scale
        )
        scores = scores.reshape(TILE * QPK, slot_total, TILE)
        mask = valid[None, :, None] & (not_diagonal[None, :, None] | causal[:, None, :])
        scores = jnp.where(mask, scores, -1e30)
        row_max = jnp.max(scores, axis=(1, 2), keepdims=True)
        unnormed = jnp.exp(scores - row_max)
        probs = unnormed / jnp.sum(unnormed, axis=(1, 2), keepdims=True)
        weights = probs.astype(jnp.bfloat16).reshape(TILE * QPK, slot_total * TILE)
        mixed = jnp.dot(weights, value_rows, preferred_element_type=jnp.float32).astype(
            jnp.bfloat16
        )
        columns = jnp.sum(probs, axis=0)
        window_hot = (window_index[:, None] == jnp.arange(window_count)[None, :]).astype(
            jnp.float32
        )
        window_sums = window_sums + jnp.sum(
            window_hot[:, :, None] * columns[: 1 + slash_count, None, :], axis=0
        )
        vertical_sums = vertical_sums + columns[1 + slash_count :]
        return ((window_sums, vertical_sums), mixed.reshape(TILE, QPK * head_dim))

    start = (
        jnp.zeros((window_count, TILE), jnp.float32),
        jnp.zeros((vertical_count, TILE), jnp.float32),
    )
    (window_sums, vertical_sums), mixed_tiles = lax.scan(per_tile, start, jnp.arange(tile_count))
    attended = mixed_tiles.reshape(tok_rows, QPK * head_dim)
    vertical_total = lax.psum(vertical_sums, "ctx")
    returned = shifted(window_sums[:tile_count], "ctx", -1)
    mine = (window_sums[tile_count:] + returned).reshape(tok_rows)
    head_total = lax.psum(mine, "head")
    return (attended, head_total / (lax.axis_size("head") * QPK), (vertical_total / QPK)[None])


def solution(mesh):
    placed = (
        P("ctx", "head"),
        P("ctx", "head"),
        P("ctx", "head"),
        P("head", None),
        P("head", None),
        P("head", "ctx"),
    )
    return jax.shard_map(
        local,
        mesh=mesh,
        in_specs=placed,
        out_specs=(P("ctx", "head"), P("ctx"), P("head", None, None)),
        check_vma=False,
    )
```

profile of v0, /device:TPU:6, one launch (start us, length us, event | category | flops | bytes accessed | tf_op | source)
XLA Modules:
  0.0 2339.7 jit_solution(10155296701002587871)
XLA Ops:
  7.2 1.1 pad_maximum_fusion
  8.3 3.9 collective-permute-start
  12.2 1.7 reshape.119
  14.1 9.2 collective-permute-done
  23.4 8.7 copy.16
  32.1 2063.3 %while.30 = (s32[]{:T(128)}, bf16[8,2,128,128]{3,2,1,0:T(8,128)(2,1)S(1)}, s32[8]{0:T(128)S(1)}, bf16[2,1024,128]{2,1,0:T(8,128)(2,1)S(1)}, s32[]{:T(128)}, /*in...) while((s32[]{:T(128)}, ...), condition=%wide.region_2.3_spmd, body=%wide.region_0.2_spmd.sunk | while | flops 65564 | bytes 655816 | solution.py:41
  36.3 263.9 %all-reduce.2.cloned.1.call-done = bf16[1,2,128,128]{3,2,1,0:T(8,128)(2,1)} async-done(((bf16[1,2,128,128]{3,2,1,0:T(8,128)(2,1)}), bf16[1,2,128,128]{3,2,1,0:T(8,128)(2,1)}) %all-reduce.2.cloned.1.call-update) | async-done | bytes 65552 | tf_op jit(solution)/shard_map/while/body/eval_jaxpr/psum | solution.py:18
  300.2 0.9 constant_dynamic-update-slice_fusion.6
  305.2 251.3 %all-reduce.2.cloned.1.call-done = bf16[1,2,128,128]{3,2,1,0:T(8,128)(2,1)} async-done(((bf16[1,2,128,128]{3,2,1,0:T(8,128)(2,1)}), bf16[1,2,128,128]{3,2,1,0:T(8,128)(2,1)}) %all-reduce.2.cloned.1.call-update) | async-done | bytes 65552 | tf_op jit(solution)/shard_map/while/body/eval_jaxpr/psum | solution.py:18
  556.5 0.9 constant_dynamic-update-slice_fusion.6
  561.6 251.3 %all-reduce.2.cloned.1.call-done = bf16[1,2,128,128]{3,2,1,0:T(8,128)(2,1)} async-done(((bf16[1,2,128,128]{3,2,1,0:T(8,128)(2,1)}), bf16[1,2,128,128]{3,2,1,0:T(8,128)(2,1)}) %all-reduce.2.cloned.1.call-update) | async-done | bytes 65552 | tf_op jit(solution)/shard_map/while/body/eval_jaxpr/psum | solution.py:18
  812.9 0.9 constant_dynamic-update-slice_fusion.6
  817.9 251.3 %all-reduce.2.cloned.1.call-done = bf16[1,2,128,128]{3,2,1,0:T(8,128)(2,1)} async-done(((bf16[1,2,128,128]{3,2,1,0:T(8,128)(2,1)}), bf16[1,2,128,128]{3,2,1,0:T(8,128)(2,1)}) %all-reduce.2.cloned.1.call-update) | async-done | bytes 65552 | tf_op jit(solution)/shard_map/while/body/eval_jaxpr/psum | solution.py:18
  1069.2 0.9 constant_dynamic-update-slice_fusion.6
  1074.2 251.3 %all-reduce.2.cloned.1.call-done = bf16[1,2,128,128]{3,2,1,0:T(8,128)(2,1)} async-done(((bf16[1,2,128,128]{3,2,1,0:T(8,128)(2,1)}), bf16[1,2,128,128]{3,2,1,0:T(8,128)(2,1)}) %all-reduce.2.cloned.1.call-update) | async-done | bytes 65552 | tf_op jit(solution)/shard_map/while/body/eval_jaxpr/psum | solution.py:18
  1325.5 0.9 constant_dynamic-update-slice_fusion.6
  1330.6 251.3 %all-reduce.2.cloned.1.call-done = bf16[1,2,128,128]{3,2,1,0:T(8,128)(2,1)} async-done(((bf16[1,2,128,128]{3,2,1,0:T(8,128)(2,1)}), bf16[1,2,128,128]{3,2,1,0:T(8,128)(2,1)}) %all-reduce.2.cloned.1.call-update) | async-done | bytes 65552 | tf_op jit(solution)/shard_map/while/body/eval_jaxpr/psum | solution.py:18
  1581.9 0.9 constant_dynamic-update-slice_fusion.6
  1586.9 251.3 %all-reduce.2.cloned.1.call-done = bf16[1,2,128,128]{3,2,1,0:T(8,128)(2,1)} async-done(((bf16[1,2,128,128]{3,2,1,0:T(8,128)(2,1)}), bf16[1,2,128,128]{3,2,1,0:T(8,128)(2,1)}) %all-reduce.2.cloned.1.call-update) | async-done | bytes 65552 | tf_op jit(solution)/shard_map/while/body/eval_jaxpr/psum | solution.py:18
  1838.2 0.9 constant_dynamic-update-slice_fusion.6
  1843.3 251.3 %all-reduce.2.cloned.1.call-done = bf16[1,2,128,128]{3,2,1,0:T(8,128)(2,1)} async-done(((bf16[1,2,128,128]{3,2,1,0:T(8,128)(2,1)}), bf16[1,2,128,128]{3,2,1,0:T(8,128)(2,1)}) %all-reduce.2.cloned.1.call-update) | async-done | bytes 65552 | tf_op jit(solution)/shard_map/while/body/eval_jaxpr/psum | solution.py:18
  2094.6 0.9 constant_dynamic-update-slice_fusion.6
  2095.5 84.2 %while.31 = (s32[]{:T(128)}, f32[16,128]{1,0:T(8,128)S(1)}, f32[8,128]{1,0:T(8,128)S(1)}, bf16[8,128,512]{2,1,0:T(8,128)(2,1)}, s32[8]{0:T(128)S(1)}, /*index=5*...) while((s32[]{:T(128)}, f32[16,128]{1,0:T(8,128)S(1)}, ...), condition=%wide.region_9.10_spmd.clone, body=%wide.region_3.9_spmd.clone.sunk | while | flops 377173888 | bytes 19409076 | solution.py:108
  2099.8 1.0 gather_fusion
  2101.3 0.8 copy.21
  2102.2 0.9 fusion.46
  2103.6 0.8 fusion.48
  2105.1 0.7 constant_dynamic-update-slice_fusion.8
  2110.3 1.0 gather_fusion
  2111.9 0.8 copy.21
  2112.7 0.9 fusion.46
  2114.2 0.8 fusion.48
  2115.6 0.7 constant_dynamic-update-slice_fusion.8
  2120.9 1.0 gather_fusion
  2122.4 0.8 copy.21
  2123.2 0.9 fusion.46
  2124.7 0.8 fusion.48
  2126.1 0.7 constant_dynamic-update-slice_fusion.8
  2131.4 1.0 gather_fusion
  2132.9 0.8 copy.21
  2133.7 0.9 fusion.46
  2135.2 0.8 fusion.48
  2136.6 0.7 constant_dynamic-update-slice_fusion.8
  2141.9 1.0 gather_fusion
  2143.4 0.8 copy.21
  2144.3 0.9 fusion.46
  2145.7 0.8 fusion.48
  2147.2 0.7 constant_dynamic-update-slice_fusion.8
  2152.4 1.0 gather_fusion
  2154.0 0.8 copy.21
  2154.8 0.9 fusion.46
  2156.3 0.8 fusion.48
  2157.7 0.7 constant_dynamic-update-slice_fusion.8
  2163.0 1.0 gather_fusion
  2164.5 0.8 copy.21
  2165.3 0.9 fusion.46
  2166.8 0.8 fusion.48
  2173.5 1.0 gather_fusion
  2175.0 0.8 copy.21
  2175.9 0.9 fusion.46
  2177.3 0.8 fusion.48
  2179.7 1.3 collective-permute-start.1
  2181.0 140.6 %psum.29 = f32[8,128]{1,0:T(8,128)S(1)} all-reduce(f32[8,128]{1,0:T(8,128)S(1)} %get-tuple-element.199), channel_id=1, replica_groups=mesh['head'=8,'ctx'=64] {'ctx'}, use_global_device_ids=true, to_apply=%region_11.12 | all-reduce | flops 1024 | bytes 8192 | tf_op jit(solution)/shard_map/psum | solution.py:110
  2322.2 10.0 psum.28
  (257 shorter events, 45.1 us)
Async XLA Ops:
  7.2 16.2 copy-start.1
  7.2 16.1 copy-start
  8.3 15.0 collective-permute-start
  12.2 19.9 copy-start.2
  14.1 2081.4 %copy-start.3 = (s32[1,2]{1,0:T(1,128)S(1)}, s32[1,2]{1,0:T(1,128)}, u32[]{:S(2)}) copy-start(s32[1,2]{1,0:T(1,128)} %param.14) | copy-start | bytes 28
  14.1 2081.4 %copy-start.4 = (s32[1,8]{1,0:T(1,128)S(1)}, s32[1,8]{1,0:T(1,128)}, u32[]{:S(2)}) copy-start(s32[1,8]{1,0:T(1,128)} %param.15) | copy-start | bytes 100
  32.1 268.1 %all-reduce.2.cloned.1.call-start = ((), (), s32[]{:S(2)}) async-start(), calls=%async_computation | async-start | bytes 131072 | tf_op jit(solution)/shard_map/while/body/eval_jaxpr/psum | solution.py:18
  301.0 255.5 %all-reduce.2.cloned.1.call-start = ((), (), s32[]{:S(2)}) async-start(), calls=%async_computation | async-start | bytes 131072 | tf_op jit(solution)/shard_map/while/body/eval_jaxpr/psum | solution.py:18
  557.4 255.5 %all-reduce.2.cloned.1.call-start = ((), (), s32[]{:S(2)}) async-start(), calls=%async_computation | async-start | bytes 131072 | tf_op jit(solution)/shard_map/while/body/eval_jaxpr/psum | solution.py:18
  813.7 255.5 %all-reduce.2.cloned.1.call-start = ((), (), s32[]{:S(2)}) async-start(), calls=%async_computation | async-start | bytes 131072 | tf_op jit(solution)/shard_map/while/body/eval_jaxpr/psum | solution.py:18
  1070.1 255.5 %all-reduce.2.cloned.1.call-start = ((), (), s32[]{:S(2)}) async-start(), calls=%async_computation | async-start | bytes 131072 | tf_op jit(solution)/shard_map/while/body/eval_jaxpr/psum | solution.py:18
  1326.4 255.5 %all-reduce.2.cloned.1.call-start = ((), (), s32[]{:S(2)}) async-start(), calls=%async_computation | async-start | bytes 131072 | tf_op jit(solution)/shard_map/while/body/eval_jaxpr/psum | solution.py:18
  1582.7 255.5 %all-reduce.2.cloned.1.call-start = ((), (), s32[]{:S(2)}) async-start(), calls=%async_computation | async-start | bytes 131072 | tf_op jit(solution)/shard_map/while/body/eval_jaxpr/psum | solution.py:18
  1839.1 255.5 %all-reduce.2.cloned.1.call-start = ((), (), s32[]{:S(2)}) async-start(), calls=%async_computation | async-start | bytes 131072 | tf_op jit(solution)/shard_map/while/body/eval_jaxpr/psum | solution.py:18
  2179.7 142.5 %collective-permute-start.1 = (f32[8,128]{1,0:T(8,128)S(1)}, f32[8,128]{1,0:T(8,128)S(1)}, u32[]{:S(2)}, u32[]{:S(2)}) collective-permute-start(f32[8,128]{1,0:T(8,128)S(1)} %slice.37), channel_id=1, source_target_pairs={{1,0},{2,1},{3,2},{4,3},{5,4},{6,5},{7,6},{8,7},{9,8},{10,9},{11,1... | collective-permute-start | bytes 12296 | tf_op jit(solution)/shard_map/ppermute | solution.py:13
Sparse Core Ops, SparseCore 0:
  36.4 263.7 all-reduce.1
  305.3 251.1 all-reduce.1
  561.7 251.1 all-reduce.1
  818.0 251.1 all-reduce.1
  1074.4 251.1 all-reduce.1
  1330.7 251.1 all-reduce.1
  1587.0 251.1 all-reduce.1
  1843.4 251.1 all-reduce.1
where the time goes:
time: 2340 us
  waiting for transfers between devices  2030 us (87%)
  blocking collectives  151 us (6%)
  local copies, waits for them, and re-layouts  56.8 us (2%)
  loops' own time  41.5 us (2%)
  other arithmetic  27 us (1%)
    psum x8, waiting for transfers between devices, spread(): return lax.psum(kept, axis)  2020 us
    psum x1, blocking collectives, local(): vertical_total = lax.psum(vertical_sums, 'ctx')  141 us
  transfers between devices with their start and end apart: 10, of which 9 were waited for; matrix products, arithmetic and copies ran while one was open for 0% of the time, Pallas kernels for 0%

commit v1 on v0

v1 whole, which is shorter than its diff:
```python
import functools
import math

import jax
import jax.numpy as jnp
from jax import lax
from jax.experimental import pallas as pl
from jax.experimental.pallas import tpu as pltpu
from jax.sharding import PartitionSpec as P

MESH = pl.DeviceIdType.MESH
QPK = 4
TILE = 128
HD = 128
NV = 8
NT = 8
ROWS = QPK * TILE
NG = 2
G = NV // NG
NY = 4
NL = 4
NH = 4
HEADS = 8
CTX = NY * NL * NH
HIDE = -1e30
RATE = HD ** -0.5 * math.log2(math.e)
F32 = jnp.float32
BF16 = jnp.bfloat16


def dot_nt(a, b):
    return lax.dot_general(a, b, (((1,), (1,)), ((), ())), preferred_element_type=F32)


def kernel(vert, slash, keep, q_hbm, k_hbm, v_hbm, att_hbm, col_ref, ver_ref,
           q, ko, vo, kw, vw, kvert, vvert, att, causal, ebuf_a, ebuf_b, mx, acc, win, vs,
           s1, r1a, r1b, s2, r2a, r2b, s3, r3a, r3b, full,
           hs, hr, rw, v1, v2, v3,
           in_sem, out_sem, slash_s, slash_r, ex_s, ex_r, t_s, t_r, h_s, h_r):
    head = lax.axis_index("head")
    ctx = lax.axis_index("ctx")
    y = ctx // (NL * NH)
    zh = (ctx // NL) % NH
    zl = ctx % NL

    def at(a, b, c):
        return (head, a * (NL * NH) + b * NL + c)

    y_peers = [((y + k) % NY, at((y + k) % NY, zh, zl)) for k in (1, 2, 3)]
    l_peers = [((zl + k) % NL, at(y, zh, (zl + k) % NL)) for k in (1, 2, 3)]
    h_peers = [((zh + k) % NH, at(y, (zh + k) % NH, zl)) for k in (1, 2, 3)]
    heads = [((head + k) % HEADS, ((head + k) % HEADS, ctx)) for k in range(1, HEADS)]
    after = (head, (ctx + 1) % CTX)
    before = (head, (ctx + CTX - 1) % CTX)

    barrier = pltpu.get_barrier_semaphore()
    greeted = [p for _, p in y_peers + l_peers + h_peers + heads] + [after, before]
    for p in greeted:
        pl.semaphore_signal(barrier, inc=1, device_id=p, device_id_type=MESH)

    loads = [
        pltpu.make_async_copy(k_hbm, ko, in_sem.at[0]),
        pltpu.make_async_copy(v_hbm, vo, in_sem.at[1]),
        pltpu.make_async_copy(q_hbm, q, in_sem.at[2]),
        pltpu.make_async_copy(k_hbm, kw.at[pl.ds(NT, NT)], in_sem.at[3]),
        pltpu.make_async_copy(v_hbm, vw.at[pl.ds(NT, NT)], in_sem.at[4]),
    ]
    for c in loads:
        c.start()

    def remote(src, dst, ss, rs, p):
        return pltpu.make_async_remote_copy(
            src_ref=src, dst_ref=dst, send_sem=ss, recv_sem=rs, device_id=p, device_id_type=MESH
        )

    row = lax.broadcasted_iota(jnp.int32, (ROWS, HD), 0) % TILE
    lane = lax.broadcasted_iota(jnp.int32, (ROWS, HD), 1)
    causal[...] = jnp.where((lane == 0) | (lane > row), 1.0, 0.0).astype(BF16)
    win[...] = jnp.zeros_like(win)
    vs[...] = jnp.zeros_like(vs)

    loads[0].wait()
    loads[1].wait()
    for j in range(NV):
        g, jj = divmod(j, G)
        for part, ref in ((0, ko), (1, vo)):
            tile = ref[vert[0, j] & (NT - 1)]
            for half in range(2):
                s1[g, 2 * part + half, jj] = tile[64 * half:64 * half + 64]
    r1 = (r1a, r1b)
    r2 = (r2a, r2b)
    r3 = (r3a, r3b)
    for g in range(NG):
        r1[g][y] = s1[g, y]

    pl.semaphore_wait(barrier, len(greeted))

    def stage(g, number, peers, src, dst):
        base = (g * 5 + number) * 3
        return [
            remote(src(i), dst(i), ex_s.at[base + n], ex_r.at[base + n], p)
            for n, (i, p) in enumerate(peers)
        ]

    steps = {}
    for g in range(NG):
        steps[g, 0] = stage(g, 0, y_peers, lambda i: s1.at[g, i], lambda i: r1[g].at[y])
        for c in steps[g, 0]:
            c.start()
    slash_copies = [
        remote(ko, kw.at[pl.ds(0, NT)], slash_s.at[0], slash_r.at[0], after),
        remote(vo, vw.at[pl.ds(0, NT)], slash_s.at[1], slash_r.at[1], after),
    ]
    for c in slash_copies:
        c.start()

    def owner(j, low, count):
        return (vert[0, j] >> low) & (count - 1)

    def arrived(g, number):
        for c in steps[g, number]:
            c.wait_recv()

    for g in range(NG):
        arrived(g, 0)
        for jj in range(G):
            src = owner(g * G + jj, 7, NY)
            block = r1[g][src, jj]
            for r in range(NL):
                s2[g, r, jj] = block[16 * r:16 * r + 16]
        r2[g][zl] = s2[g, zl]
        steps[g, 1] = stage(g, 1, l_peers, lambda i: s2.at[g, i], lambda i: r2[g].at[zl])
        for c in steps[g, 1]:
            c.start()
    for g in range(NG):
        arrived(g, 1)
        for jj in range(G):
            s3[g, jj] = r2[g][owner(g * G + jj, 3, NL), jj]
        r3[g][zh] = s3[g]
        steps[g, 2] = stage(g, 2, h_peers, lambda i: s3.at[g], lambda i: r3[g].at[zh])
        for c in steps[g, 2]:
            c.start()

    for c in loads[2:]:
        c.wait()
    for c in slash_copies:
        c.wait_recv()
    key_row = lax.broadcasted_iota(jnp.int32, (TILE, HD), 0)
    key_lane = lax.broadcasted_iota(jnp.int32, (TILE, HD), 1)
    near = slash[0, 1]

    def stacked(i):
        rows = q[pl.ds(pl.multiple_of(i * TILE, TILE), TILE), :]
        return jnp.concatenate([rows[:, h * HD:(h + 1) * HD] for h in range(QPK)], axis=0)

    def soft(scores):
        top = jnp.max(scores, axis=1, keepdims=True)
        return top, jnp.exp2((scores - top) * RATE).astype(BF16)

    def mixed(weights, value_rows):
        ones = jnp.ones(value_rows.shape, BF16)
        return jnp.dot(weights, jnp.concatenate([value_rows, ones], axis=1), preferred_element_type=F32)

    def first(i, _):
        t = ctx * NT + i
        keys = jnp.concatenate([kw[NT + i], kw[i], kw[NT + i - near]], axis=0)
        values = jnp.concatenate([vw[NT + i], vw[i], vw[NT + i - near]], axis=0)
        diagonal = jnp.where((key_row == key_lane) & (key_lane > 0), HIDE, 0.0).astype(BF16)
        far_bias = jnp.where((key_lane == 0) & (key_lane + t < slash[0, 0]), HIDE, 0.0).astype(BF16)
        near_bias = jnp.where((key_lane == 0) & (key_lane + t < near), HIDE, 0.0).astype(BF16)
        bias = jnp.concatenate([diagonal, far_bias, near_bias], axis=0)
        query = jnp.concatenate([stacked(i), causal[...]], axis=1)
        scores = dot_nt(query, jnp.concatenate([keys, bias], axis=1))
        top, weights = soft(scores)
        ebuf_a[i] = weights
        mx[0, i] = jnp.broadcast_to(top, (ROWS, HD))
        acc[i] = mixed(weights, values)
        return 0

    lax.fori_loop(0, NT, first, 0)

    for g in range(NG):
        arrived(g, 2)
        for jj in range(G):
            full[g, 4 * y + zl, jj] = r3[g][owner(g * G + jj, 5, NH), jj]
        steps[g, 3] = stage(g, 3, l_peers, lambda i: full.at[g, 4 * y + zl], lambda i: full.at[g, 4 * y + zl])
        for c in steps[g, 3]:
            c.start()
    for g in range(NG):
        arrived(g, 3)
        mine = pl.ds(4 * y, 4)
        steps[g, 4] = stage(g, 4, y_peers, lambda i: full.at[g, mine], lambda i: full.at[g, mine])
        for c in steps[g, 4]:
            c.start()

    lanes8 = lax.broadcasted_iota(jnp.int32, (8, HD), 1)
    ids = jnp.zeros((8, HD), jnp.int32)
    for j in range(NV):
        ids = jnp.where(lanes8 == j, vert[0, j], ids)
    slot_row = lax.broadcasted_iota(jnp.int32, (G * TILE, HD), 0) // TILE
    slot_lane = lax.broadcasted_iota(jnp.int32, (G * TILE, HD), 1)

    def flags(i):
        t = ctx * NT + i
        valid = (lanes8 < keep[0, i]) & (ids < t) & (ids != t - slash[0, 0]) & (ids != t - near)
        flag = jnp.where(valid | (lanes8 >= NV), 0.0, 1.0)
        return jnp.broadcast_to(flag[:1], (ROWS, HD)).astype(BF16)

    for g in range(NG):
        arrived(g, 4)
        for jj in range(G):
            kvert[g, jj] = jnp.concatenate([full[g, p, jj] for p in range(8)], axis=0)
            vvert[g, jj] = jnp.concatenate([full[g, 8 + p, jj] for p in range(8)], axis=0)
        bias = jnp.where(slot_row + g * G == slot_lane, HIDE, 0.0).astype(BF16)

        def vertical(i, _):
            keys = kvert[g].reshape(G * TILE, HD)
            values = vvert[g].reshape(G * TILE, HD)
            query = jnp.concatenate([stacked(i), flags(i)], axis=1)
            scores = dot_nt(query, jnp.concatenate([keys, bias], axis=1))
            top, weights = soft(scores)
            ebuf_b[g, i] = weights
            new = jnp.broadcast_to(top, (ROWS, HD))
            old = mx[g, i]
            top = jnp.maximum(old, new)
            mx[g + 1, i] = top
            before_scale = jnp.exp2((old - top) * RATE)
            now_scale = jnp.exp2((new - top) * RATE)
            part = mixed(weights, values)
            held = acc[i]
            acc[i] = jnp.concatenate(
                [held[:, :HD] * before_scale + part[:, :HD] * now_scale,
                 held[:, HD:] * before_scale + part[:, HD:] * now_scale], axis=1)
            hs[g, i] = new
            return 0

        lax.fori_loop(0, NT, vertical, 0)

    lane_id = lax.broadcasted_iota(jnp.int32, (ROWS, HD), 1)
    win_row = lax.broadcasted_iota(jnp.int32, (2 * NT, TILE), 0)
    vs_row = lax.broadcasted_iota(jnp.int32, (NV, TILE), 0)

    def finish(i, _):
        held = acc[i]
        inverse = 1.0 / held[:, HD:]
        out = (held[:, :HD] * inverse).astype(BF16)
        here = pl.ds(pl.multiple_of(i * TILE, TILE), TILE)
        att[here, :] = jnp.concatenate([out[h * TILE:(h + 1) * TILE] for h in range(QPK)], axis=1)
        pltpu.make_async_copy(att.at[here, :], att_hbm.at[here, :], out_sem.at[i]).start()
        top = mx[NG, i]
        factors = jnp.exp2((mx[0, i] - top) * RATE) * inverse
        for g in range(NG):
            factors = jnp.where(lane_id == g + 1, jnp.exp2((hs[g, i] - top) * RATE) * inverse, factors)
        turned = jnp.transpose(factors)[:8]
        high = turned.astype(BF16)
        low = (turned - high.astype(F32)).astype(BF16)
        rows = jnp.concatenate([high, low], axis=0)

        def sums(weights, which):
            both = jnp.dot(rows, weights, preferred_element_type=F32)
            return both[which:which + 1] + both[8 + which:9 + which]

        near_sums = sums(ebuf_a[i], 0)
        add = jnp.where(win_row == NT + i, near_sums[:, :TILE], 0.0)
        add = add + jnp.where(win_row == i, near_sums[:, TILE:2 * TILE], 0.0)
        add = add + jnp.where(win_row == NT + i - near, near_sums[:, 2 * TILE:], 0.0)
        win[...] += add
        total = vs[...]
        for g in range(NG):
            part = sums(ebuf_b[g, i], g + 1)
            for jj in range(G):
                total = total + jnp.where(vs_row == g * G + jj, part[:, jj * TILE:(jj + 1) * TILE], 0.0)
        vs[...] = total
        return 0

    lax.fori_loop(0, NT, finish, 0)

    to_before = remote(win.at[pl.ds(0, NT)], rw, h_s.at[7], h_r.at[7], before)
    to_before.start()
    v1[y] = vs[...]
    c1 = [remote(vs, v1.at[y], t_s.at[n], t_r.at[n], p) for n, (_, p) in enumerate(y_peers)]
    for c in c1:
        c.start()
    to_before.wait_recv()
    hr[head] = win[NT:] + rw[...]
    ch = [remote(hr.at[head], hr.at[head], h_s.at[n], h_r.at[n], p) for n, (_, p) in enumerate(heads)]
    for c in ch:
        c.start()
    for c in c1:
        c.wait_recv()
    v2[zl] = (v1[0] + v1[1]) + (v1[2] + v1[3])
    c2 = [remote(v2.at[zl], v2.at[zl], t_s.at[3 + n], t_r.at[3 + n], p) for n, (_, p) in enumerate(l_peers)]
    for c in c2:
        c.start()
    for c in c2:
        c.wait_recv()
    v3[zh] = (v2[0] + v2[1]) + (v2[2] + v2[3])
    c3 = [remote(v3.at[zh], v3.at[zh], t_s.at[6 + n], t_r.at[6 + n], p) for n, (_, p) in enumerate(h_peers)]
    for c in c3:
        c.start()
    for c in ch:
        c.wait_recv()
    total = hr[0]
    for n in range(1, HEADS):
        total = total + hr[n]
    col_ref[...] = total * (1.0 / (HEADS * QPK))
    for c in c3:
        c.wait_recv()
    ver_ref[0] = ((v3[0] + v3[1]) + (v3[2] + v3[3])) * (1.0 / QPK)

    for c in [c for group in steps.values() for c in group] + slash_copies + [to_before] + c1 + c2 + c3 + ch:
        c.wait_send()
    for i in range(NT):
        here = pl.ds(i * TILE, TILE)
        pltpu.make_async_copy(att.at[here, :], att_hbm.at[here, :], out_sem.at[i]).wait()


def local(queries, keys, values, vertical_ids, slash_offsets, keep_counts):
    rows = keys.shape[0]
    smem = pl.BlockSpec(memory_space=pltpu.SMEM)
    vmem = pl.BlockSpec(memory_space=pltpu.VMEM)
    hbm = pl.BlockSpec(memory_space=pl.ANY)
    dma = pltpu.SemaphoreType.DMA
    attended, column, vertical = pl.pallas_call(
        kernel,
        out_shape=(
            jax.ShapeDtypeStruct(queries.shape, BF16),
            jax.ShapeDtypeStruct((NT, TILE), F32),
            jax.ShapeDtypeStruct((1, NV, TILE), F32),
        ),
        in_specs=[smem, smem, smem, hbm, hbm, hbm],
        out_specs=(hbm, vmem, vmem),
        scratch_shapes=[
            pltpu.VMEM((rows, QPK * HD), BF16),
            *[pltpu.VMEM((NT, TILE, HD), BF16) for _ in range(2)],
            *[pltpu.VMEM((2 * NT, TILE, HD), BF16) for _ in range(2)],
            *[pltpu.VMEM((NG, G, TILE, HD), BF16) for _ in range(2)],
            pltpu.VMEM((rows, QPK * HD), BF16),
            pltpu.VMEM((ROWS, HD), BF16),
            pltpu.VMEM((NT, ROWS, 3 * TILE), BF16),
            pltpu.VMEM((NG, NT, ROWS, G * TILE), BF16),
            pltpu.VMEM((NG + 1, NT, ROWS, HD), F32),
            pltpu.VMEM((NT, ROWS, 2 * HD), F32),
            pltpu.VMEM((2 * NT, TILE), F32),
            pltpu.VMEM((NV, TILE), F32),
            pltpu.VMEM((NG, NY, G, 64, HD), BF16),
            *[pltpu.VMEM((NY, G, 64, HD), BF16) for _ in range(2)],
            pltpu.VMEM((NG, NL, G, 16, HD), BF16),
            *[pltpu.VMEM((NL, G, 16, HD), BF16) for _ in range(2)],
            pltpu.VMEM((NG, G, 16, HD), BF16),
            *[pltpu.VMEM((NH, G, 16, HD), BF16) for _ in range(2)],
            pltpu.VMEM((NG, 16, G, 16, HD), BF16),
            pltpu.VMEM((NG, NT, ROWS, HD), F32),
            pltpu.VMEM((HEADS, NT, TILE), F32),
            pltpu.VMEM((NT, TILE), F32),
            pltpu.VMEM((NY, NV, TILE), F32),
            pltpu.VMEM((NL, NV, TILE), F32),
            pltpu.VMEM((NH, NV, TILE), F32),
            dma((5,)), dma((NT,)), dma((2,)), dma((2,)),
            dma((NG * 15,)), dma((NG * 15,)), dma((9,)), dma((9,)), dma((8,)), dma((8,)),
        ],
        compiler_params=pltpu.CompilerParams(
            collective_id=0, has_side_effects=True, vmem_limit_bytes=56 << 20
        ),
    )(vertical_ids, slash_offsets, keep_counts, queries, keys.reshape(NT, TILE, HD), values.reshape(NT, TILE, HD))
    return attended, column.reshape(rows), vertical


def solution(mesh):
    placed = (
        P("ctx", "head"),
        P("ctx", "head"),
        P("ctx", "head"),
        P("head", None),
        P("head", None),
        P("head", "ctx"),
    )
    return jax.shard_map(
        local,
        mesh=mesh,
        in_specs=placed,
        out_specs=(P("ctx", "head"), P("ctx"), P("head", None, None)),
        check_vma=False,
    )
```

time: 2340 us -> 90.6 us (0.04)
  waiting for transfers between devices: 2030 us -> 0 us
  blocking collectives: 151 us -> 0 us
  Pallas kernels: 0 us -> 86.2 us
  local copies, waits for them, and re-layouts: 56.8 us -> 3.53 us
  loops' own time: 41.5 us -> 0 us
  other arithmetic: 27 us -> 0 us
    psum x8 -> x0, waiting for transfers between devices: 2020 us -> none  [spread(): return lax.psum(kept, axis)]
    psum x2 -> x0, blocking collectives: 151 us -> none  [the longest x1 141 us: local(): vertical_total = lax.psum(vertical_sums, 'ctx')]
    pallas_call x0 -> x1, Pallas kernels: none -> 86.2 us  [local(): pl.pallas_call(kernel, out_shape=(jax.ShapeDtypeStruct(queries.shape, BF1...]
    another operation x2 -> x0, loops' own time: 41.5 us -> none  [the longest x1 22.6 us: local(): lax.fori_loop(0, vertical_count, fetch_tile, jnp.zeros((vertical_count, 2...]
  transfers between devices with their start and end apart: 10 -> 0, of which waited for: 9 -> 0; matrix products, arithmetic and copies ran while one was open for 0% -> 0% of each run, Pallas kernels for 0% -> 0%
where the time goes in v1:
time: 90.6 us; the launch traced here: 90.3 us
  Pallas kernels  86.2 us (95%)
  local copies, waits for them, and re-layouts  3.53 us (4%)
    pallas_call x1, Pallas kernels, local(): pl.pallas_call(kernel, out_shape=(jax.ShapeDtypeStruct(queries.shape, BF1...  86.2 us
    unnamed x7, local copies, waits for them, and re-layouts  3.53 us

profile of v1, /device:TPU:6, one launch (start us, length us, event | category | flops | bytes accessed | tf_op | source)
XLA Modules:
  0.0 90.3 jit_solution(8878015123942807383)
XLA Ops:
  0.6 86.2 %shard_map.85 = (bf16[1024,512]{1,0:T(8,128)(2,1)}, f32[8,128]{1,0:T(8,128)}, f32[1,8,128]{2,1,0:T(8,128)}) custom-call(s32[1,8]{1,0:T(1,128)} %vert.1, s32[1,2]{1,0:T(1,128)} %slash.1, s32[1,8]{1,0:T(1,128)} %keep.1, bf16[1024,512]{1,0:T(8,128)(2,1)} %q_hbm.1, bf16[8,128,128]{2,1,0:T(8,128)(2,1)} %bitcast.3, bf16[8,128,128]{2,1,0:T(8,128)(2,1)} %bitcast.4), custom_call_target="tpu_custom_call" | custom-call | tf_op jit(solution)/shard_map/pallas_call | solution.py:324
  86.8 0.0 copy-start.1
  86.8 2.3 %copy.12 = bf16[1024,512]{1,0:T(8,128)(2,1)} copy(bf16[1024,512]{1,0:T(8,128)(2,1)} %get-tuple-element.12) | data formatting | bytes 2097152
  89.1 0.0 copy-done.1
  89.1 0.0 copy-start
  89.1 0.6 copy.13
  89.7 0.1 copy-done
  89.8 0.6 copy.14
Async XLA Ops:
  86.8 2.3 %copy-start.1 = (f32[8,128]{1,0:T(8,128)S(1)}, f32[8,128]{1,0:T(8,128)}, u32[]{:S(2)}) copy-start(f32[8,128]{1,0:T(8,128)} %get-tuple-element.7) | copy-start | bytes 12292
  89.1 0.7 copy-start

commit v2 on v1

--- a/solution.py
+++ b/solution.py
@@ -24,6 +24,9 @@
 CTX = NY * NL * NH
 HIDE = -1e30
 RATE = HD ** -0.5 * math.log2(math.e)
+NEAR = (-1, -2, 1)
+SLASH_K = 0
+SLASH_V = 2
 F32 = jnp.float32
 BF16 = jnp.bfloat16
 
@@ -32,29 +35,35 @@
     return lax.dot_general(a, b, (((1,), (1,)), ((), ())), preferred_element_type=F32)
 
 
-def kernel(vert, slash, keep, q_hbm, k_hbm, v_hbm, att_hbm, col_ref, ver_ref,
-           q, ko, vo, kw, vw, kvert, vvert, att, causal, ebuf_a, ebuf_b, mx, acc, win, vs,
+def kernel(vert, slash, keep, q_hbm, k_hbm, v_hbm, att, col_ref, ver_ref,
+           q, ko, vo, kw, vw, kvert, vvert, causal, ebuf_a, ebuf_b, mx, acc, win, vs,
            s1, r1a, r1b, s2, r2a, r2b, s3, r3a, r3b, full,
-           hs, hr, rw, v1, v2, v3,
-           in_sem, out_sem, slash_s, slash_r, ex_s, ex_r, t_s, t_r, h_s, h_r):
+           hr, rw, v1, v2, v3,
+           in_sem, slash_s, slash_r, ex_s, ex_r, last_s, last_r, t_s, t_r, h_s, h_r):
     head = lax.axis_index("head")
     ctx = lax.axis_index("ctx")
     y = ctx // (NL * NH)
     zh = (ctx // NL) % NH
     zl = ctx % NL
+    z = ctx % (NL * NH)
 
     def at(a, b, c):
         return (head, a * (NL * NH) + b * NL + c)
+
+    def along(k):
+        return (head, y * (NL * NH) + (z + k + NL * NH) % (NL * NH))
 
     y_peers = [((y + k) % NY, at((y + k) % NY, zh, zl)) for k in (1, 2, 3)]
     l_peers = [((zl + k) % NL, at(y, zh, (zl + k) % NL)) for k in (1, 2, 3)]
     h_peers = [((zh + k) % NH, at(y, (zh + k) % NH, zl)) for k in (1, 2, 3)]
+    n_peers = [((zl + k + NL) % NL, along(k)) for k in NEAR]
     heads = [((head + k) % HEADS, ((head + k) % HEADS, ctx)) for k in range(1, HEADS)]
     after = (head, (ctx + 1) % CTX)
     before = (head, (ctx + CTX - 1) % CTX)
 
     barrier = pltpu.get_barrier_semaphore()
-    greeted = [p for _, p in y_peers + l_peers + h_peers + heads] + [after, before]
+    greeted = [p for _, p in h_peers + y_peers + l_peers + heads] + [after, before]
+    greeted += [along(k) for k in (-2, -1, 1, 2)]
     for p in greeted:
         pl.semaphore_signal(barrier, inc=1, device_id=p, device_id_type=MESH)
 
@@ -85,13 +94,20 @@
         g, jj = divmod(j, G)
         for part, ref in ((0, ko), (1, vo)):
             tile = ref[vert[0, j] & (NT - 1)]
-            for half in range(2):
-                s1[g, 2 * part + half, jj] = tile[64 * half:64 * half + 64]
+            for piece in range(8):
+                of_y, of_l = divmod(8 * part + piece, NL)
+                rows = tile[16 * piece:16 * piece + 16]
+                if g == 0:
+                    s1[g, of_y, jj, 16 * of_l:16 * of_l + 16] = rows
+                else:
+                    s1[g, of_l, jj, 16 * of_y:16 * of_y + 16] = rows
     r1 = (r1a, r1b)
     r2 = (r2a, r2b)
     r3 = (r3a, r3b)
-    for g in range(NG):
-        r1[g][y] = s1[g, y]
+    mine = ((y, zl), (zl, y))
+    peers = ((y_peers, n_peers), (n_peers, y_peers))
+    for g in range(NG):
+        r1[g][mine[g][0]] = s1[g, mine[g][0]]
 
     pl.semaphore_wait(barrier, len(greeted))
 
@@ -104,15 +120,21 @@
 
     steps = {}
     for g in range(NG):
-        steps[g, 0] = stage(g, 0, y_peers, lambda i: s1.at[g, i], lambda i: r1[g].at[y])
+        steps[g, 0] = stage(g, 0, peers[g][0], lambda i: s1.at[g, i], lambda i: r1[g].at[mine[g][0]])
         for c in steps[g, 0]:
             c.start()
+    lower = pl.ds(0, NT)
     slash_copies = [
-        remote(ko, kw.at[pl.ds(0, NT)], slash_s.at[0], slash_r.at[0], after),
-        remote(vo, vw.at[pl.ds(0, NT)], slash_s.at[1], slash_r.at[1], after),
+        remote(ko, kw.at[lower], slash_s.at[0], slash_r.at[0], after),
+        remote(vo, vw.at[lower], slash_s.at[1], slash_r.at[1], after),
     ]
-    for c in slash_copies:
-        c.start()
+
+    def send_slash(number):
+        for c, when in zip(slash_copies, (SLASH_K, SLASH_V)):
+            if when == number:
+                c.start()
+
+    send_slash(0)
 
     def owner(j, low, count):
         return (vert[0, j] >> low) & (count - 1)
@@ -124,27 +146,31 @@
     for g in range(NG):
         arrived(g, 0)
         for jj in range(G):
-            src = owner(g * G + jj, 7, NY)
+            j = g * G + jj
+            src = owner(j, 7, NY) if g == 0 else owner(j, 3, NL)
             block = r1[g][src, jj]
-            for r in range(NL):
-                s2[g, r, jj] = block[16 * r:16 * r + 16]
-        r2[g][zl] = s2[g, zl]
-        steps[g, 1] = stage(g, 1, l_peers, lambda i: s2.at[g, i], lambda i: r2[g].at[zl])
+            for n in range(4):
+                s2[g, n, jj] = block[16 * n:16 * n + 16]
+        r2[g][mine[g][1]] = s2[g, mine[g][1]]
+        steps[g, 1] = stage(g, 1, peers[g][1], lambda i: s2.at[g, i], lambda i: r2[g].at[mine[g][1]])
         for c in steps[g, 1]:
             c.start()
+    send_slash(1)
     for g in range(NG):
         arrived(g, 1)
         for jj in range(G):
-            s3[g, jj] = r2[g][owner(g * G + jj, 3, NL), jj]
+            j = g * G + jj
+            src = owner(j, 3, NL) if g == 0 else owner(j, 7, NY)
+            s3[g, jj] = r2[g][src, jj]
         r3[g][zh] = s3[g]
         steps[g, 2] = stage(g, 2, h_peers, lambda i: s3.at[g], lambda i: r3[g].at[zh])
         for c in steps[g, 2]:
             c.start()
+    send_slash(2)
 
     for c in loads[2:]:
         c.wait()
-    for c in slash_copies:
-        c.wait_recv()
+    slash_copies[0].wait_recv()
     key_row = lax.broadcasted_iota(jnp.int32, (TILE, HD), 0)
     key_lane = lax.broadcasted_iota(jnp.int32, (TILE, HD), 1)
     near = slash[0, 1]
@@ -164,7 +190,6 @@
     def first(i, _):
         t = ctx * NT + i
         keys = jnp.concatenate([kw[NT + i], kw[i], kw[NT + i - near]], axis=0)
-        values = jnp.concatenate([vw[NT + i], vw[i], vw[NT + i - near]], axis=0)
         diagonal = jnp.where((key_row == key_lane) & (key_lane > 0), HIDE, 0.0).astype(BF16)
         far_bias = jnp.where((key_lane == 0) & (key_lane + t < slash[0, 0]), HIDE, 0.0).astype(BF16)
         near_bias = jnp.where((key_lane == 0) & (key_lane + t < near), HIDE, 0.0).astype(BF16)
@@ -174,24 +199,36 @@
         top, weights = soft(scores)
         ebuf_a[i] = weights
         mx[0, i] = jnp.broadcast_to(top, (ROWS, HD))
-        acc[i] = mixed(weights, values)
         return 0
 
-    lax.fori_loop(0, NT, first, 0)
-
+    lax.fori_loop(0, NT, first, 0, unroll=4)
+
+    piece = 4 * y + zl
     for g in range(NG):
         arrived(g, 2)
         for jj in range(G):
-            full[g, 4 * y + zl, jj] = r3[g][owner(g * G + jj, 5, NH), jj]
-        steps[g, 3] = stage(g, 3, l_peers, lambda i: full.at[g, 4 * y + zl], lambda i: full.at[g, 4 * y + zl])
+            j = g * G + jj
+            of = owner(j, 3, NL * NH)
+            gathered = (of + ((zl - of + 2) & (NL - 1)) - 2) & (NL * NH - 1)
+            full[g, piece, jj] = r3[g][gathered >> 2, jj]
+        steps[g, 3] = stage(g, 3, peers[g][1], lambda i: full.at[g, piece], lambda i: full.at[g, piece])
         for c in steps[g, 3]:
             c.start()
+    send_slash(3)
     for g in range(NG):
         arrived(g, 3)
-        mine = pl.ds(4 * y, 4)
-        steps[g, 4] = stage(g, 4, y_peers, lambda i: full.at[g, mine], lambda i: full.at[g, mine])
+        if g == 0:
+            block = pl.ds(4 * y, 4)
+            steps[g, 4] = stage(g, 4, y_peers, lambda i: full.at[g, block], lambda i: full.at[g, block])
+        else:
+            steps[g, 4] = [
+                remote(full.at[g, 4 * n + zl], full.at[g, 4 * n + zl], last_s.at[3 * n + k], last_r.at[3 * n + k], p)
+                for n in range(NY)
+                for k, (_, p) in enumerate(n_peers)
+            ]
         for c in steps[g, 4]:
             c.start()
+    send_slash(4)
 
     lanes8 = lax.broadcasted_iota(jnp.int32, (8, HD), 1)
     ids = jnp.zeros((8, HD), jnp.int32)
@@ -220,37 +257,31 @@
             scores = dot_nt(query, jnp.concatenate([keys, bias], axis=1))
             top, weights = soft(scores)
             ebuf_b[g, i] = weights
-            new = jnp.broadcast_to(top, (ROWS, HD))
-            old = mx[g, i]
-            top = jnp.maximum(old, new)
-            mx[g + 1, i] = top
-            before_scale = jnp.exp2((old - top) * RATE)
-            now_scale = jnp.exp2((new - top) * RATE)
-            part = mixed(weights, values)
-            held = acc[i]
-            acc[i] = jnp.concatenate(
-                [held[:, :HD] * before_scale + part[:, :HD] * now_scale,
-                 held[:, HD:] * before_scale + part[:, HD:] * now_scale], axis=1)
-            hs[g, i] = new
+            mx[g + 1, i] = jnp.broadcast_to(top, (ROWS, HD))
+            acc[g + 1, i] = mixed(weights, values)
             return 0
 
-        lax.fori_loop(0, NT, vertical, 0)
+        lax.fori_loop(0, NT, vertical, 0, unroll=4)
+
+    slash_copies[1].wait_recv()
 
     lane_id = lax.broadcasted_iota(jnp.int32, (ROWS, HD), 1)
     win_row = lax.broadcasted_iota(jnp.int32, (2 * NT, TILE), 0)
     vs_row = lax.broadcasted_iota(jnp.int32, (NV, TILE), 0)
 
     def finish(i, _):
-        held = acc[i]
-        inverse = 1.0 / held[:, HD:]
-        out = (held[:, :HD] * inverse).astype(BF16)
-        here = pl.ds(pl.multiple_of(i * TILE, TILE), TILE)
-        att[here, :] = jnp.concatenate([out[h * TILE:(h + 1) * TILE] for h in range(QPK)], axis=1)
-        pltpu.make_async_copy(att.at[here, :], att_hbm.at[here, :], out_sem.at[i]).start()
-        top = mx[NG, i]
-        factors = jnp.exp2((mx[0, i] - top) * RATE) * inverse
-        for g in range(NG):
-            factors = jnp.where(lane_id == g + 1, jnp.exp2((hs[g, i] - top) * RATE) * inverse, factors)
+        values = jnp.concatenate([vw[NT + i], vw[i], vw[NT + i - near]], axis=0)
+        acc[0, i] = mixed(ebuf_a[i], values)
+        tops = [mx[x, i] for x in range(NG + 1)]
+        top = functools.reduce(jnp.maximum, tops)
+        scales = [jnp.exp2((t - top) * RATE) for t in tops]
+        inverse = 1.0 / sum(acc[x, i, :, HD:] * scales[x] for x in range(NG + 1))
+        scales = [f * inverse for f in scales]
+        for x in range(NG + 1):
+            mx[x, i] = scales[x]
+        factors = scales[0]
+        for x in range(1, NG + 1):
+            factors = jnp.where(lane_id == x, scales[x], factors)
         turned = jnp.transpose(factors)[:8]
         high = turned.astype(BF16)
         low = (turned - high.astype(F32)).astype(BF16)
@@ -273,7 +304,7 @@
         vs[...] = total
         return 0
 
-    lax.fori_loop(0, NT, finish, 0)
+    lax.fori_loop(0, NT, finish, 0, unroll=4)
 
     to_before = remote(win.at[pl.ds(0, NT)], rw, h_s.at[7], h_r.at[7], before)
     to_before.start()
@@ -281,17 +312,26 @@
     c1 = [remote(vs, v1.at[y], t_s.at[n], t_r.at[n], p) for n, (_, p) in enumerate(y_peers)]
     for c in c1:
         c.start()
+
+    def normalise(i, _):
+        out = sum(acc[x, i, :, :HD] * mx[x, i] for x in range(NG + 1)).astype(BF16)
+        here = pl.ds(pl.multiple_of(i * TILE, TILE), TILE)
+        att[here, :] = jnp.concatenate([out[h * TILE:(h + 1) * TILE] for h in range(QPK)], axis=1)
+        return 0
+
     to_before.wait_recv()
     hr[head] = win[NT:] + rw[...]
     ch = [remote(hr.at[head], hr.at[head], h_s.at[n], h_r.at[n], p) for n, (_, p) in enumerate(heads)]
     for c in ch:
         c.start()
+    lax.fori_loop(0, NT // 2, normalise, 0)
     for c in c1:
         c.wait_recv()
     v2[zl] = (v1[0] + v1[1]) + (v1[2] + v1[3])
     c2 = [remote(v2.at[zl], v2.at[zl], t_s.at[3 + n], t_r.at[3 + n], p) for n, (_, p) in enumerate(l_peers)]
     for c in c2:
         c.start()
+    lax.fori_loop(NT // 2, NT, normalise, 0)
     for c in c2:
         c.wait_recv()
     v3[zh] = (v2[0] + v2[1]) + (v2[2] + v2[3])
@@ -310,9 +350,6 @@
 
     for c in [c for group in steps.values() for c in group] + slash_copies + [to_before] + c1 + c2 + c3 + ch:
         c.wait_send()
-    for i in range(NT):
-        here = pl.ds(i * TILE, TILE)
-        pltpu.make_async_copy(att.at[here, :], att_hbm.at[here, :], out_sem.at[i]).wait()
 
 
 def local(queries, keys, values, vertical_ids, slash_offsets, keep_counts):
@@ -324,40 +361,38 @@
     attended, column, vertical = pl.pallas_call(
         kernel,
         out_shape=(
-            jax.ShapeDtypeStruct(queries.shape, BF16),
-            jax.ShapeDtypeStruct((NT, TILE), F32),
-            jax.ShapeDtypeStruct((1, NV, TILE), F32),
+            pltpu.VMEM(queries.shape, BF16),
+            pltpu.VMEM((NT, TILE), F32),
+            pltpu.VMEM((1, NV, TILE), F32),
         ),
         in_specs=[smem, smem, smem, hbm, hbm, hbm],
-        out_specs=(hbm, vmem, vmem),
+        out_specs=(vmem, vmem, vmem),
         scratch_shapes=[
             pltpu.VMEM((rows, QPK * HD), BF16),
             *[pltpu.VMEM((NT, TILE, HD), BF16) for _ in range(2)],
             *[pltpu.VMEM((2 * NT, TILE, HD), BF16) for _ in range(2)],
             *[pltpu.VMEM((NG, G, TILE, HD), BF16) for _ in range(2)],
-            pltpu.VMEM((rows, QPK * HD), BF16),
             pltpu.VMEM((ROWS, HD), BF16),
             pltpu.VMEM((NT, ROWS, 3 * TILE), BF16),
             pltpu.VMEM((NG, NT, ROWS, G * TILE), BF16),
             pltpu.VMEM((NG + 1, NT, ROWS, HD), F32),
-            pltpu.VMEM((NT, ROWS, 2 * HD), F32),
+            pltpu.VMEM((NG + 1, NT, ROWS, 2 * HD), F32),
             pltpu.VMEM((2 * NT, TILE), F32),
             pltpu.VMEM((NV, TILE), F32),
-            pltpu.VMEM((NG, NY, G, 64, HD), BF16),
+            pltpu.VMEM((NG, 4, G, 64, HD), BF16),
             *[pltpu.VMEM((NY, G, 64, HD), BF16) for _ in range(2)],
             pltpu.VMEM((NG, NL, G, 16, HD), BF16),
             *[pltpu.VMEM((NL, G, 16, HD), BF16) for _ in range(2)],
             pltpu.VMEM((NG, G, 16, HD), BF16),
             *[pltpu.VMEM((NH, G, 16, HD), BF16) for _ in range(2)],
             pltpu.VMEM((NG, 16, G, 16, HD), BF16),
-            pltpu.VMEM((NG, NT, ROWS, HD), F32),
             pltpu.VMEM((HEADS, NT, TILE), F32),
             pltpu.VMEM((NT, TILE), F32),
             pltpu.VMEM((NY, NV, TILE), F32),
             pltpu.VMEM((NL, NV, TILE), F32),
             pltpu.VMEM((NH, NV, TILE), F32),
-            dma((5,)), dma((NT,)), dma((2,)), dma((2,)),
-            dma((NG * 15,)), dma((NG * 15,)), dma((9,)), dma((9,)), dma((8,)), dma((8,)),
+            dma((5,)), dma((2,)), dma((2,)),
+            dma((NG * 15,)), dma((NG * 15,)), dma((12,)), dma((12,)), dma((9,)), dma((9,)), dma((8,)), dma((8,)),
         ],
         compiler_params=pltpu.CompilerParams(
             collective_id=0, has_side_effects=True, vmem_limit_bytes=56 << 20

time: 90.6 us -> 77.1 us (0.85)
  Pallas kernels: 86.2 us -> 74.1 us
  local copies, waits for them, and re-layouts: 3.53 us -> 2.16 us
    pallas_call x1, Pallas kernels: 86.2 us -> 74.1 us  [local(): pl.pallas_call(kernel, out_shape=(pltpu.VMEM(queries.shape, BF16), pltpu....]
    unnamed x7 -> x3, local copies, waits for them, and re-layouts: 3.53 us -> 2.16 us
where the time goes in v2:
time: 77.1 us; the launch traced here: 76.9 us
  Pallas kernels  74.1 us (96%)
  local copies, waits for them, and re-layouts  2.16 us (3%)
    pallas_call x1, Pallas kernels, local(): pl.pallas_call(kernel, out_shape=(pltpu.VMEM(queries.shape, BF16), pltpu....  74.1 us
    unnamed x3, local copies, waits for them, and re-layouts  2.16 us

profile of v2, /device:TPU:6, one launch (start us, length us, event | category | flops | bytes accessed | tf_op | source)
XLA Modules:
  0.0 76.9 jit_solution(14879672418454263840)
XLA Ops:
  0.6 74.1 %shard_map.85 = (bf16[1024,512]{1,0:T(8,128)(2,1)S(1)}, f32[8,128]{1,0:T(8,128)S(1)}, f32[1,8,128]{2,1,0:T(8,128)S(1)}) custom-call(s32[1,8]{1,0:T(1,128)} %vert.1, s32[1,2]{1,0:T(1,128)} %slash.1, s32[1,8]{1,0:T(1,128)} %keep.1, bf16[1024,512]{1,0:T(8,128)(2,1)} %q_hbm.1, bf16[8,128,128]{2,1,0:T(8,128)(2,1)} %bitcast.4, bf16[8,128,128]{2,1,0:T(8,128)(2,1)} %bitcast.5), custom_call_target="tpu_custom_call" | custom-call | tf_op jit(solution)/shard_map/pallas_call | solution.py:361
  74.7 1.0 %copy.12 = bf16[1024,512]{1,0:T(8,128)(2,1)} copy(bf16[1024,512]{1,0:T(8,128)(2,1)S(1)} %get-tuple-element.9) | data formatting | bytes 2097152
  75.7 0.6 copy.13
  76.3 0.6 copy.14

commit v3 on v2

--- a/solution.py
+++ b/solution.py
@@ -36,10 +36,10 @@
 
 
 def kernel(vert, slash, keep, q_hbm, k_hbm, v_hbm, att, col_ref, ver_ref,
-           q, ko, vo, kw, vw, kvert, vvert, causal, ebuf_a, ebuf_b, mx, acc, win, vs,
+           q, ko, vo, kw, vw, kvert, vvert, causal, ebuf_a, ebuf_b, mx, acc0, acc, sc, win, vs,
            s1, r1a, r1b, s2, r2a, r2b, s3, r3a, r3b, full,
-           hr, rw, v1, v2, v3,
-           in_sem, slash_s, slash_r, ex_s, ex_r, last_s, last_r, t_s, t_r, h_s, h_r):
+           hr, rw, v1, vz,
+           in_sem, slash_s, slash_r, ex_s, ex_r, t_s, t_r, h_s, h_r):
     head = lax.axis_index("head")
     ctx = lax.axis_index("ctx")
     y = ctx // (NL * NH)
@@ -54,7 +54,6 @@
         return (head, y * (NL * NH) + (z + k + NL * NH) % (NL * NH))
 
     y_peers = [((y + k) % NY, at((y + k) % NY, zh, zl)) for k in (1, 2, 3)]
-    l_peers = [((zl + k) % NL, at(y, zh, (zl + k) % NL)) for k in (1, 2, 3)]
     h_peers = [((zh + k) % NH, at(y, (zh + k) % NH, zl)) for k in (1, 2, 3)]
     n_peers = [((zl + k + NL) % NL, along(k)) for k in NEAR]
     heads = [((head + k) % HEADS, ((head + k) % HEADS, ctx)) for k in range(1, HEADS)]
@@ -62,8 +61,8 @@
     before = (head, (ctx + CTX - 1) % CTX)
 
     barrier = pltpu.get_barrier_semaphore()
-    greeted = [p for _, p in h_peers + y_peers + l_peers + heads] + [after, before]
-    greeted += [along(k) for k in (-2, -1, 1, 2)]
+    z_peers = [along(k) for k in (8, 7, -7, 6, -6, 5, -5, 4, -4, 3, -3, 2, -2, 1, -1)]
+    greeted = z_peers + [p for _, p in y_peers + heads] + [after, before]
     for p in greeted:
         pl.semaphore_signal(barrier, inc=1, device_id=p, device_id_type=MESH)
 
@@ -85,8 +84,6 @@
     row = lax.broadcasted_iota(jnp.int32, (ROWS, HD), 0) % TILE
     lane = lax.broadcasted_iota(jnp.int32, (ROWS, HD), 1)
     causal[...] = jnp.where((lane == 0) | (lane > row), 1.0, 0.0).astype(BF16)
-    win[...] = jnp.zeros_like(win)
-    vs[...] = jnp.zeros_like(vs)
 
     loads[0].wait()
     loads[1].wait()
@@ -203,32 +200,34 @@
 
     lax.fori_loop(0, NT, first, 0, unroll=4)
 
-    piece = 4 * y + zl
+    piece = (4 * y + zl, 4 * zl + y)
     for g in range(NG):
         arrived(g, 2)
         for jj in range(G):
             j = g * G + jj
             of = owner(j, 3, NL * NH)
             gathered = (of + ((zl - of + 2) & (NL - 1)) - 2) & (NL * NH - 1)
-            full[g, piece, jj] = r3[g][gathered >> 2, jj]
-        steps[g, 3] = stage(g, 3, peers[g][1], lambda i: full.at[g, piece], lambda i: full.at[g, piece])
+            full[g, piece[g], jj] = r3[g][gathered >> 2, jj]
+        steps[g, 3] = stage(g, 3, peers[g][1], lambda i: full.at[g, piece[g]], lambda i: full.at[g, piece[g]])
         for c in steps[g, 3]:
             c.start()
     send_slash(3)
     for g in range(NG):
         arrived(g, 3)
-        if g == 0:
-            block = pl.ds(4 * y, 4)
-            steps[g, 4] = stage(g, 4, y_peers, lambda i: full.at[g, block], lambda i: full.at[g, block])
-        else:
-            steps[g, 4] = [
-                remote(full.at[g, 4 * n + zl], full.at[g, 4 * n + zl], last_s.at[3 * n + k], last_r.at[3 * n + k], p)
-                for n in range(NY)
-                for k, (_, p) in enumerate(n_peers)
-            ]
+        block = pl.ds(4 * mine[g][0], 4)
+        steps[g, 4] = stage(g, 4, peers[g][0], lambda i: full.at[g, block], lambda i: full.at[g, block])
         for c in steps[g, 4]:
             c.start()
     send_slash(4)
+
+    slash_copies[1].wait_recv()
+
+    def mix(i, _):
+        values = jnp.concatenate([vw[NT + i], vw[i], vw[NT + i - near]], axis=0)
+        acc0[i] = mixed(ebuf_a[i], values)
+        return 0
+
+    lax.fori_loop(0, NT, mix, 0, unroll=4)
 
     lanes8 = lax.broadcasted_iota(jnp.int32, (8, HD), 1)
     ids = jnp.zeros((8, HD), jnp.int32)
@@ -246,8 +245,9 @@
     for g in range(NG):
         arrived(g, 4)
         for jj in range(G):
-            kvert[g, jj] = jnp.concatenate([full[g, p, jj] for p in range(8)], axis=0)
-            vvert[g, jj] = jnp.concatenate([full[g, 8 + p, jj] for p in range(8)], axis=0)
+            order = [p if g == 0 else 4 * (p % 4) + p // 4 for p in range(16)]
+            kvert[g, jj] = jnp.concatenate([full[g, p, jj] for p in order[:8]], axis=0)
+            vvert[g, jj] = jnp.concatenate([full[g, p, jj] for p in order[8:]], axis=0)
         bias = jnp.where(slot_row + g * G == slot_lane, HIDE, 0.0).astype(BF16)
 
         def vertical(i, _):
@@ -258,27 +258,27 @@
             top, weights = soft(scores)
             ebuf_b[g, i] = weights
             mx[g + 1, i] = jnp.broadcast_to(top, (ROWS, HD))
-            acc[g + 1, i] = mixed(weights, values)
+            acc[g, i] = mixed(weights, values)
             return 0
 
-        lax.fori_loop(0, NT, vertical, 0, unroll=4)
-
-    slash_copies[1].wait_recv()
+        lax.fori_loop(0, NT, vertical, 0, unroll=8)
 
     lane_id = lax.broadcasted_iota(jnp.int32, (ROWS, HD), 1)
     win_row = lax.broadcasted_iota(jnp.int32, (2 * NT, TILE), 0)
     vs_row = lax.broadcasted_iota(jnp.int32, (NV, TILE), 0)
 
-    def finish(i, _):
-        values = jnp.concatenate([vw[NT + i], vw[i], vw[NT + i - near]], axis=0)
-        acc[0, i] = mixed(ebuf_a[i], values)
+    def finish(i, carry):
+        window_sums, vertical_sums = carry
         tops = [mx[x, i] for x in range(NG + 1)]
         top = functools.reduce(jnp.maximum, tops)
         scales = [jnp.exp2((t - top) * RATE) for t in tops]
-        inverse = 1.0 / sum(acc[x, i, :, HD:] * scales[x] for x in range(NG + 1))
+        total = acc0[i, :, HD:] * scales[0]
+        for g in range(NG):
+            total = total + acc[g, i, :, HD:] * scales[g + 1]
+        inverse = 1.0 / total
         scales = [f * inverse for f in scales]
         for x in range(NG + 1):
-            mx[x, i] = scales[x]
+            sc[x, i] = scales[x]
         factors = scales[0]
         for x in range(1, NG + 1):
             factors = jnp.where(lane_id == x, scales[x], factors)
@@ -295,16 +295,15 @@
         add = jnp.where(win_row == NT + i, near_sums[:, :TILE], 0.0)
         add = add + jnp.where(win_row == i, near_sums[:, TILE:2 * TILE], 0.0)
         add = add + jnp.where(win_row == NT + i - near, near_sums[:, 2 * TILE:], 0.0)
-        win[...] += add
-        total = vs[...]
         for g in range(NG):
             part = sums(ebuf_b[g, i], g + 1)
             for jj in range(G):
-                total = total + jnp.where(vs_row == g * G + jj, part[:, jj * TILE:(jj + 1) * TILE], 0.0)
-        vs[...] = total
-        return 0
-
-    lax.fori_loop(0, NT, finish, 0, unroll=4)
+                here = vs_row == g * G + jj
+                vertical_sums = vertical_sums + jnp.where(here, part[:, jj * TILE:(jj + 1) * TILE], 0.0)
+        return window_sums + add, vertical_sums
+
+    zeros = (jnp.zeros((2 * NT, TILE), F32), jnp.zeros((NV, TILE), F32))
+    win[...], vs[...] = lax.fori_loop(0, NT, finish, zeros, unroll=8)
 
     to_before = remote(win.at[pl.ds(0, NT)], rw, h_s.at[7], h_r.at[7], before)
     to_before.start()
@@ -314,7 +313,10 @@
         c.start()
 
     def normalise(i, _):
-        out = sum(acc[x, i, :, :HD] * mx[x, i] for x in range(NG + 1)).astype(BF16)
+        out = acc0[i, :, :HD] * sc[0, i]
+        for g in range(NG):
+            out = out + acc[g, i, :, :HD] * sc[g + 1, i]
+        out = out.astype(BF16)
         here = pl.ds(pl.multiple_of(i * TILE, TILE), TILE)
         att[here, :] = jnp.concatenate([out[h * TILE:(h + 1) * TILE] for h in range(QPK)], axis=1)
         return 0
@@ -327,28 +329,27 @@
     lax.fori_loop(0, NT // 2, normalise, 0)
     for c in c1:
         c.wait_recv()
-    v2[zl] = (v1[0] + v1[1]) + (v1[2] + v1[3])
-    c2 = [remote(v2.at[zl], v2.at[zl], t_s.at[3 + n], t_r.at[3 + n], p) for n, (_, p) in enumerate(l_peers)]
+    vz[z] = (v1[0] + v1[1]) + (v1[2] + v1[3])
+    c2 = [remote(vz.at[z], vz.at[z], t_s.at[3 + n], t_r.at[3 + n], p) for n, p in enumerate(z_peers)]
     for c in c2:
         c.start()
     lax.fori_loop(NT // 2, NT, normalise, 0)
-    for c in c2:
-        c.wait_recv()
-    v3[zh] = (v2[0] + v2[1]) + (v2[2] + v2[3])
-    c3 = [remote(v3.at[zh], v3.at[zh], t_s.at[6 + n], t_r.at[6 + n], p) for n, (_, p) in enumerate(h_peers)]
-    for c in c3:
-        c.start()
     for c in ch:
         c.wait_recv()
     total = hr[0]
     for n in range(1, HEADS):
         total = total + hr[n]
     col_ref[...] = total * (1.0 / (HEADS * QPK))
-    for c in c3:
+    for c in [c for group in steps.values() for c in group] + slash_copies + [to_before] + c1:
+        c.wait_send()
+    for c in c2:
         c.wait_recv()
-    ver_ref[0] = ((v3[0] + v3[1]) + (v3[2] + v3[3])) * (1.0 / QPK)
-
-    for c in [c for group in steps.values() for c in group] + slash_copies + [to_before] + c1 + c2 + c3 + ch:
+    total = vz[0]
+    for n in range(1, NL * NH):
+        total = total + vz[n]
+    ver_ref[0] = total * (1.0 / QPK)
+
+    for c in c2 + ch:
         c.wait_send()
 
 
@@ -376,7 +377,9 @@
             pltpu.VMEM((NT, ROWS, 3 * TILE), BF16),
             pltpu.VMEM((NG, NT, ROWS, G * TILE), BF16),
             pltpu.VMEM((NG + 1, NT, ROWS, HD), F32),
-            pltpu.VMEM((NG + 1, NT, ROWS, 2 * HD), F32),
+            pltpu.VMEM((NT, ROWS, 2 * HD), F32),
+            pltpu.VMEM((NG, NT, ROWS, 2 * HD), F32),
+            pltpu.VMEM((NG + 1, NT, ROWS, HD), F32),
             pltpu.VMEM((2 * NT, TILE), F32),
             pltpu.VMEM((NV, TILE), F32),
             pltpu.VMEM((NG, 4, G, 64, HD), BF16),
@@ -389,10 +392,9 @@
             pltpu.VMEM((HEADS, NT, TILE), F32),
             pltpu.VMEM((NT, TILE), F32),
             pltpu.VMEM((NY, NV, TILE), F32),
-            pltpu.VMEM((NL, NV, TILE), F32),
-            pltpu.VMEM((NH, NV, TILE), F32),
+            pltpu.VMEM((NL * NH, NV, TILE), F32),
             dma((5,)), dma((2,)), dma((2,)),
-            dma((NG * 15,)), dma((NG * 15,)), dma((12,)), dma((12,)), dma((9,)), dma((9,)), dma((8,)), dma((8,)),
+            dma((NG * 15,)), dma((NG * 15,)), dma((18,)), dma((18,)), dma((8,)), dma((8,)),
         ],
         compiler_params=pltpu.CompilerParams(
             collective_id=0, has_side_effects=True, vmem_limit_bytes=56 << 20

time: 77.1 us -> 69.8 us (0.905)
  Pallas kernels: 74.1 us -> 66.8 us
    pallas_call x1, Pallas kernels: 74.1 us -> 66.8 us  [local(): pl.pallas_call(kernel, out_shape=(pltpu.VMEM(queries.shape, BF16), pltpu....]
where the time goes in v3:
time: 69.8 us; the launch traced here: 69.6 us
  Pallas kernels  66.8 us (96%)
  local copies, waits for them, and re-layouts  2.16 us (3%)
    pallas_call x1, Pallas kernels, local(): pl.pallas_call(kernel, out_shape=(pltpu.VMEM(queries.shape, BF16), pltpu....  66.8 us
    unnamed x3, local copies, waits for them, and re-layouts  2.16 us

profile of v3, /device:TPU:6, one launch (start us, length us, event | category | flops | bytes accessed | tf_op | source)
XLA Modules:
  0.0 69.6 jit_solution(18345226780232929748)
XLA Ops:
  0.6 66.8 %shard_map.85 = (bf16[1024,512]{1,0:T(8,128)(2,1)S(1)}, f32[8,128]{1,0:T(8,128)S(1)}, f32[1,8,128]{2,1,0:T(8,128)S(1)}) custom-call(s32[1,8]{1,0:T(1,128)} %vert.1, s32[1,2]{1,0:T(1,128)} %slash.1, s32[1,8]{1,0:T(1,128)} %keep.1, bf16[1024,512]{1,0:T(8,128)(2,1)} %q_hbm.1, bf16[8,128,128]{2,1,0:T(8,128)(2,1)} %bitcast.4, bf16[8,128,128]{2,1,0:T(8,128)(2,1)} %bitcast.5), custom_call_target="tpu_custom_call" | custom-call | tf_op jit(solution)/shard_map/pallas_call | solution.py:362
  67.5 1.0 %copy.12 = bf16[1024,512]{1,0:T(8,128)(2,1)} copy(bf16[1024,512]{1,0:T(8,128)(2,1)S(1)} %get-tuple-element.9) | data formatting | bytes 2097152
  68.4 0.6 copy.13
  69.0 0.6 copy.14

commit v4 on v3

--- a/solution.py
+++ b/solution.py
@@ -25,7 +25,7 @@
 HIDE = -1e30
 RATE = HD ** -0.5 * math.log2(math.e)
 NEAR = (-1, -2, 1)
-SLASH_K = 0
+SLASH_K = 1
 SLASH_V = 2
 F32 = jnp.float32
 BF16 = jnp.bfloat16
@@ -35,8 +35,8 @@
     return lax.dot_general(a, b, (((1,), (1,)), ((), ())), preferred_element_type=F32)
 
 
-def kernel(vert, slash, keep, q_hbm, k_hbm, v_hbm, att, col_ref, ver_ref,
-           q, ko, vo, kw, vw, kvert, vvert, causal, ebuf_a, ebuf_b, mx, acc0, acc, sc, win, vs,
+def kernel(vert_hbm, slash_hbm, keep_hbm, q_hbm, k_hbm, v_hbm, att, col_ref, ver_ref,
+           vert, slash, keep, q, ko, vo, kw, vw, kvert, vvert, causal, ebuf_a, ebuf_b, mx, acc0, acc, sc, win, vs,
            s1, r1a, r1b, s2, r2a, r2b, s3, r3a, r3b, full,
            hr, rw, v1, vz,
            in_sem, slash_s, slash_r, ex_s, ex_r, t_s, t_r, h_s, h_r):
@@ -73,7 +73,12 @@
         pltpu.make_async_copy(k_hbm, kw.at[pl.ds(NT, NT)], in_sem.at[3]),
         pltpu.make_async_copy(v_hbm, vw.at[pl.ds(NT, NT)], in_sem.at[4]),
     ]
-    for c in loads:
+    small = [
+        pltpu.make_async_copy(vert_hbm, vert, in_sem.at[5]),
+        pltpu.make_async_copy(slash_hbm, slash, in_sem.at[6]),
+        pltpu.make_async_copy(keep_hbm, keep, in_sem.at[7]),
+    ]
+    for c in small + loads:
         c.start()
 
     def remote(src, dst, ss, rs, p):
@@ -85,8 +90,8 @@
     lane = lax.broadcasted_iota(jnp.int32, (ROWS, HD), 1)
     causal[...] = jnp.where((lane == 0) | (lane > row), 1.0, 0.0).astype(BF16)
 
-    loads[0].wait()
-    loads[1].wait()
+    for c in small + loads[:2]:
+        c.wait()
     for j in range(NV):
         g, jj = divmod(j, G)
         for part, ref in ((0, ko), (1, vo)):
@@ -165,6 +170,26 @@
             c.start()
     send_slash(2)
 
+    piece = (4 * y + zl, 4 * zl + y)
+    for g in range(NG):
+        arrived(g, 2)
+        for jj in range(G):
+            j = g * G + jj
+            of = owner(j, 3, NL * NH)
+            gathered = (of + ((zl - of + 2) & (NL - 1)) - 2) & (NL * NH - 1)
+            full[g, piece[g], jj] = r3[g][gathered >> 2, jj]
+        steps[g, 3] = stage(g, 3, peers[g][1], lambda i: full.at[g, piece[g]], lambda i: full.at[g, piece[g]])
+        for c in steps[g, 3]:
+            c.start()
+    send_slash(3)
+    for g in range(NG):
+        arrived(g, 3)
+        block = pl.ds(4 * mine[g][0], 4)
+        steps[g, 4] = stage(g, 4, peers[g][0], lambda i: full.at[g, block], lambda i: full.at[g, block])
+        for c in steps[g, 4]:
+            c.start()
+    send_slash(4)
+
     for c in loads[2:]:
         c.wait()
     slash_copies[0].wait_recv()
@@ -199,26 +224,6 @@
         return 0
 
     lax.fori_loop(0, NT, first, 0, unroll=4)
-
-    piece = (4 * y + zl, 4 * zl + y)
-    for g in range(NG):
-        arrived(g, 2)
-        for jj in range(G):
-            j = g * G + jj
-            of = owner(j, 3, NL * NH)
-            gathered = (of + ((zl - of + 2) & (NL - 1)) - 2) & (NL * NH - 1)
-            full[g, piece[g], jj] = r3[g][gathered >> 2, jj]
-        steps[g, 3] = stage(g, 3, peers[g][1], lambda i: full.at[g, piece[g]], lambda i: full.at[g, piece[g]])
-        for c in steps[g, 3]:
-            c.start()
-    send_slash(3)
-    for g in range(NG):
-        arrived(g, 3)
-        block = pl.ds(4 * mine[g][0], 4)
-        steps[g, 4] = stage(g, 4, peers[g][0], lambda i: full.at[g, block], lambda i: full.at[g, block])
-        for c in steps[g, 4]:
-            c.start()
-    send_slash(4)
 
     slash_copies[1].wait_recv()
 
@@ -355,7 +360,6 @@
 
 def local(queries, keys, values, vertical_ids, slash_offsets, keep_counts):
     rows = keys.shape[0]
-    smem = pl.BlockSpec(memory_space=pltpu.SMEM)
     vmem = pl.BlockSpec(memory_space=pltpu.VMEM)
     hbm = pl.BlockSpec(memory_space=pl.ANY)
     dma = pltpu.SemaphoreType.DMA
@@ -366,9 +370,10 @@
             pltpu.VMEM((NT, TILE), F32),
             pltpu.VMEM((1, NV, TILE), F32),
         ),
-        in_specs=[smem, smem, smem, hbm, hbm, hbm],
+        in_specs=[hbm] * 6,
         out_specs=(vmem, vmem, vmem),
         scratch_shapes=[
+            *[pltpu.SMEM(a.shape, jnp.int32) for a in (vertical_ids, slash_offsets, keep_counts)],
             pltpu.VMEM((rows, QPK * HD), BF16),
             *[pltpu.VMEM((NT, TILE, HD), BF16) for _ in range(2)],
             *[pltpu.VMEM((2 * NT, TILE, HD), BF16) for _ in range(2)],
@@ -393,7 +398,7 @@
             pltpu.VMEM((NT, TILE), F32),
             pltpu.VMEM((NY, NV, TILE), F32),
             pltpu.VMEM((NL * NH, NV, TILE), F32),
-            dma((5,)), dma((2,)), dma((2,)),
+            dma((8,)), dma((2,)), dma((2,)),
             dma((NG * 15,)), dma((NG * 15,)), dma((18,)), dma((18,)), dma((8,)), dma((8,)),
         ],
         compiler_params=pltpu.CompilerParams(

time: 69.8 us -> 67.6 us (0.968)
  Pallas kernels: 66.8 us -> 64.6 us
    pallas_call x1, Pallas kernels: 66.8 us -> 64.6 us  [local(): pl.pallas_call(kernel, out_shape=(pltpu.VMEM(queries.shape, BF16), pltpu....]
where the time goes in v4:
time: 67.6 us; the launch traced here: 67.4 us
  Pallas kernels  64.6 us (96%)
  local copies, waits for them, and re-layouts  2.16 us (3%)
    pallas_call x1, Pallas kernels, local(): pl.pallas_call(kernel, out_shape=(pltpu.VMEM(queries.shape, BF16), pltpu....  64.6 us
    unnamed x3, local copies, waits for them, and re-layouts  2.16 us

profile of v4, /device:TPU:6, one launch (start us, length us, event | category | flops | bytes accessed | tf_op | source)
XLA Modules:
  0.0 67.4 jit_solution(5981882253248373716)
XLA Ops:
  0.6 64.6 %shard_map.85 = (bf16[1024,512]{1,0:T(8,128)(2,1)S(1)}, f32[8,128]{1,0:T(8,128)S(1)}, f32[1,8,128]{2,1,0:T(8,128)S(1)}) custom-call(s32[1,8]{1,0:T(1,128)} %vert_hbm.1, s32[1,2]{1,0:T(1,128)} %slash_hbm.1, s32[1,8]{1,0:T(1,128)} %keep_hbm.1, bf16[1024,512]{1,0:T(8,128)(2,1)} %q_hbm.1, bf16[8,128,128]{2,1,0:T(8,128)(2,1)} %bitcast.4, bf16[8,128,128]{2,1,0:T(8,128)(2,1)} %bitcast.5), custom_call_target="tpu_custom_call" | custom-call | tf_op jit(solution)/shard_map/pallas_call | solution.py:366
  65.3 1.0 %copy.12 = bf16[1024,512]{1,0:T(8,128)(2,1)} copy(bf16[1024,512]{1,0:T(8,128)(2,1)S(1)} %get-tuple-element.9) | data formatting | bytes 2097152
  66.3 0.6 copy.13
  66.9 0.6 copy.14

commit v5 on v4

--- a/solution.py
+++ b/solution.py
@@ -35,11 +35,11 @@
     return lax.dot_general(a, b, (((1,), (1,)), ((), ())), preferred_element_type=F32)
 
 
-def kernel(vert_hbm, slash_hbm, keep_hbm, q_hbm, k_hbm, v_hbm, att, col_ref, ver_ref,
-           vert, slash, keep, q, ko, vo, kw, vw, kvert, vvert, causal, ebuf_a, ebuf_b, mx, acc0, acc, sc, win, vs,
+def kernel(vert_hbm, slash_hbm, keep_hbm, q_hbm, k_hbm, v_hbm, att, sums_ref,
+           vert, slash, keep, q, ko, vo, kw, vw, kvert, vvert, causal, ebuf_a, ebuf_b, shares, mx, acc0, acc, sc, win, vs,
            s1, r1a, r1b, s2, r2a, r2b, s3, r3a, r3b, full,
            hr, rw, v1, vz,
-           in_sem, slash_s, slash_r, ex_s, ex_r, t_s, t_r, h_s, h_r):
+           in_sem, slash_s, slash_r, ex_s, ex_r, far_s, far_r, t_s, t_r, h_s, h_r):
     head = lax.axis_index("head")
     ctx = lax.axis_index("ctx")
     y = ctx // (NL * NH)
@@ -54,7 +54,7 @@
         return (head, y * (NL * NH) + (z + k + NL * NH) % (NL * NH))
 
     y_peers = [((y + k) % NY, at((y + k) % NY, zh, zl)) for k in (1, 2, 3)]
-    h_peers = [((zh + k) % NH, at(y, (zh + k) % NH, zl)) for k in (1, 2, 3)]
+    h_peers = [((zh + k) % NH, at(y, (zh + k) % NH, zl)) for k in (2, 1, 3)]
     n_peers = [((zl + k + NL) % NL, along(k)) for k in NEAR]
     heads = [((head + k) % HEADS, ((head + k) % HEADS, ctx)) for k in range(1, HEADS)]
     after = (head, (ctx + 1) % CTX)
@@ -122,7 +122,15 @@
 
     steps = {}
     for g in range(NG):
-        steps[g, 0] = stage(g, 0, peers[g][0], lambda i: s1.at[g, i], lambda i: r1[g].at[mine[g][0]])
+        if g == 0:
+            steps[g, 0] = stage(g, 0, peers[g][0], lambda i: s1.at[g, i], lambda i: r1[g].at[mine[g][0]])
+        else:
+            split = [(zl + NL - 1) % NL, (zl + 1) % NL] + [(zl + 2) % NL] * 2
+            slots = [pl.ds(0, G)] * 2 + [pl.ds(0, G // 2), pl.ds(G // 2, G // 2)]
+            steps[g, 0] = [
+                remote(s1.at[g, i, part], r1[g].at[zl, part], far_s.at[n], far_r.at[n], along(k))
+                for n, (i, part, k) in enumerate(zip(split, slots, (-1, 1, -2, 2)))
+            ]
         for c in steps[g, 0]:
             c.start()
     lower = pl.ds(0, NT)
@@ -175,8 +183,9 @@
         arrived(g, 2)
         for jj in range(G):
             j = g * G + jj
+            low = 1 if g == 1 and jj >= G // 2 else 2
             of = owner(j, 3, NL * NH)
-            gathered = (of + ((zl - of + 2) & (NL - 1)) - 2) & (NL * NH - 1)
+            gathered = (of + ((zl - of + low) & (NL - 1)) - low) & (NL * NH - 1)
             full[g, piece[g], jj] = r3[g][gathered >> 2, jj]
         steps[g, 3] = stage(g, 3, peers[g][1], lambda i: full.at[g, piece[g]], lambda i: full.at[g, piece[g]])
         for c in steps[g, 3]:
@@ -272,8 +281,11 @@
     win_row = lax.broadcasted_iota(jnp.int32, (2 * NT, TILE), 0)
     vs_row = lax.broadcasted_iota(jnp.int32, (NV, TILE), 0)
 
-    def finish(i, carry):
-        window_sums, vertical_sums = carry
+    def sums(rows, weights, which):
+        both = jnp.dot(rows, weights, preferred_element_type=F32)
+        return both[which:which + 1] + both[8 + which:9 + which]
+
+    def finish(i, vertical_sums):
         tops = [mx[x, i] for x in range(NG + 1)]
         top = functools.reduce(jnp.maximum, tops)
         scales = [jnp.exp2((t - top) * RATE) for t in tops]
@@ -291,30 +303,37 @@
         high = turned.astype(BF16)
         low = (turned - high.astype(F32)).astype(BF16)
         rows = jnp.concatenate([high, low], axis=0)
-
-        def sums(weights, which):
-            both = jnp.dot(rows, weights, preferred_element_type=F32)
-            return both[which:which + 1] + both[8 + which:9 + which]
-
-        near_sums = sums(ebuf_a[i], 0)
-        add = jnp.where(win_row == NT + i, near_sums[:, :TILE], 0.0)
-        add = add + jnp.where(win_row == i, near_sums[:, TILE:2 * TILE], 0.0)
-        add = add + jnp.where(win_row == NT + i - near, near_sums[:, 2 * TILE:], 0.0)
+        shares[i] = rows
+
         for g in range(NG):
-            part = sums(ebuf_b[g, i], g + 1)
+            part = sums(rows, ebuf_b[g, i], g + 1)
             for jj in range(G):
                 here = vs_row == g * G + jj
                 vertical_sums = vertical_sums + jnp.where(here, part[:, jj * TILE:(jj + 1) * TILE], 0.0)
-        return window_sums + add, vertical_sums
-
-    zeros = (jnp.zeros((2 * NT, TILE), F32), jnp.zeros((NV, TILE), F32))
-    win[...], vs[...] = lax.fori_loop(0, NT, finish, zeros, unroll=8)
-
-    to_before = remote(win.at[pl.ds(0, NT)], rw, h_s.at[7], h_r.at[7], before)
-    to_before.start()
+        return vertical_sums
+
+    vs[...] = lax.fori_loop(0, NT, finish, jnp.zeros((NV, TILE), F32), unroll=8)
+
     v1[y] = vs[...]
     c1 = [remote(vs, v1.at[y], t_s.at[n], t_r.at[n], p) for n, (_, p) in enumerate(y_peers)]
     for c in c1:
+        c.start()
+
+    def near_sums(i, window_sums):
+        part = sums(shares[i], ebuf_a[i], 0)
+        add = jnp.where(win_row == NT + i, part[:, :TILE], 0.0)
+        add = add + jnp.where(win_row == i, part[:, TILE:2 * TILE], 0.0)
+        add = add + jnp.where(win_row == NT + i - near, part[:, 2 * TILE:], 0.0)
+        return window_sums + add
+
+    win[...] = lax.fori_loop(0, NT, near_sums, jnp.zeros((2 * NT, TILE), F32), unroll=4)
+    to_before = remote(win.at[pl.ds(0, NT)], rw, h_s.at[7], h_r.at[7], before)
+    to_before.start()
+    for c in c1:
+        c.wait_recv()
+    vz[z] = (v1[0] + v1[1]) + (v1[2] + v1[3])
+    c2 = [remote(vz.at[z], vz.at[z], t_s.at[3 + n], t_r.at[3 + n], p) for n, p in enumerate(z_peers)]
+    for c in c2:
         c.start()
 
     def normalise(i, _):
@@ -326,17 +345,11 @@
         att[here, :] = jnp.concatenate([out[h * TILE:(h + 1) * TILE] for h in range(QPK)], axis=1)
         return 0
 
+    lax.fori_loop(0, NT // 2, normalise, 0)
     to_before.wait_recv()
     hr[head] = win[NT:] + rw[...]
     ch = [remote(hr.at[head], hr.at[head], h_s.at[n], h_r.at[n], p) for n, (_, p) in enumerate(heads)]
     for c in ch:
-        c.start()
-    lax.fori_loop(0, NT // 2, normalise, 0)
-    for c in c1:
-        c.wait_recv()
-    vz[z] = (v1[0] + v1[1]) + (v1[2] + v1[3])
-    c2 = [remote(vz.at[z], vz.at[z], t_s.at[3 + n], t_r.at[3 + n], p) for n, p in enumerate(z_peers)]
-    for c in c2:
         c.start()
     lax.fori_loop(NT // 2, NT, normalise, 0)
     for c in ch:
@@ -344,7 +357,7 @@
     total = hr[0]
     for n in range(1, HEADS):
         total = total + hr[n]
-    col_ref[...] = total * (1.0 / (HEADS * QPK))
+    sums_ref[0] = total * (1.0 / (HEADS * QPK))
     for c in [c for group in steps.values() for c in group] + slash_copies + [to_before] + c1:
         c.wait_send()
     for c in c2:
@@ -352,7 +365,7 @@
     total = vz[0]
     for n in range(1, NL * NH):
         total = total + vz[n]
-    ver_ref[0] = total * (1.0 / QPK)
+    sums_ref[1] = total * (1.0 / QPK)
 
     for c in c2 + ch:
         c.wait_send()
@@ -363,15 +376,14 @@
     vmem = pl.BlockSpec(memory_space=pltpu.VMEM)
     hbm = pl.BlockSpec(memory_space=pl.ANY)
     dma = pltpu.SemaphoreType.DMA
-    attended, column, vertical = pl.pallas_call(
+    attended, both = pl.pallas_call(
         kernel,
         out_shape=(
             pltpu.VMEM(queries.shape, BF16),
-            pltpu.VMEM((NT, TILE), F32),
-            pltpu.VMEM((1, NV, TILE), F32),
+            pltpu.VMEM((2, NT, TILE), F32),
         ),
         in_specs=[hbm] * 6,
-        out_specs=(vmem, vmem, vmem),
+        out_specs=(vmem, vmem),
         scratch_shapes=[
             *[pltpu.SMEM(a.shape, jnp.int32) for a in (vertical_ids, slash_offsets, keep_counts)],
             pltpu.VMEM((rows, QPK * HD), BF16),
@@ -381,6 +393,7 @@
             pltpu.VMEM((ROWS, HD), BF16),
             pltpu.VMEM((NT, ROWS, 3 * TILE), BF16),
             pltpu.VMEM((NG, NT, ROWS, G * TILE), BF16),
+            pltpu.VMEM((NT, 16, ROWS), BF16),
             pltpu.VMEM((NG + 1, NT, ROWS, HD), F32),
             pltpu.VMEM((NT, ROWS, 2 * HD), F32),
             pltpu.VMEM((NG, NT, ROWS, 2 * HD), F32),
@@ -399,13 +412,13 @@
             pltpu.VMEM((NY, NV, TILE), F32),
             pltpu.VMEM((NL * NH, NV, TILE), F32),
             dma((8,)), dma((2,)), dma((2,)),
-            dma((NG * 15,)), dma((NG * 15,)), dma((18,)), dma((18,)), dma((8,)), dma((8,)),
+            dma((NG * 15,)), dma((NG * 15,)), dma((4,)), dma((4,)), dma((18,)), dma((18,)), dma((8,)), dma((8,)),
         ],
         compiler_params=pltpu.CompilerParams(
             collective_id=0, has_side_effects=True, vmem_limit_bytes=56 << 20
         ),
     )(vertical_ids, slash_offsets, keep_counts, queries, keys.reshape(NT, TILE, HD), values.reshape(NT, TILE, HD))
-    return attended, column.reshape(rows), vertical
+    return attended, both[0].reshape(rows), both[1:]
 
 
 def solution(mesh):

time: 67.6 us -> 67.2 us (level)
    unnamed x3 -> x1, local copies, waits for them, and re-layouts: 2.16 us -> 0.97 us
where the time goes in v5:
time: 67.2 us; the launch traced here: 67 us
  Pallas kernels  64.8 us (96%)
  local copies, waits for them, and re-layouts  1.57 us (2%)
    pallas_call x1, Pallas kernels, local(): pl.pallas_call(kernel, out_shape=(pltpu.VMEM(queries.shape, BF16), pltpu....  64.8 us

profile of v5, /device:TPU:6, one launch (start us, length us, event | category | flops | bytes accessed | tf_op | source)
XLA Modules:
  0.0 67.0 jit_solution(15786589097790600896)
XLA Ops:
  0.6 64.8 %shard_map.85 = (bf16[1024,512]{1,0:T(8,128)(2,1)S(1)}, f32[2,8,128]{2,1,0:T(8,128)S(1)}) custom-call(s32[1,8]{1,0:T(1,128)} %vert_hbm.1, s32[1,2]{1,0:T(1,128)} %slash_hbm.1, s32[1,8]{1,0:T(1,128)} %keep_hbm.1, bf16[1024,512]{1,0:T(8,128)(2,1)} %q_hbm.1, bf16[8,128,128]{2,1,0:T(8,128)(2,1)} %bitcast.4, bf16[8,128,128]{2,1,0:T(8,128)(2,1)} %bitcast.5), custom_call_target="tpu_custom_call" | custom-call | tf_op jit(solution)/shard_map/pallas_call | solution.py:379
  65.5 1.0 %copy.10 = bf16[1024,512]{1,0:T(8,128)(2,1)} copy(bf16[1024,512]{1,0:T(8,128)(2,1)S(1)} %get-tuple-element.9) | data formatting | bytes 2097152
  66.4 0.6 fusion

commit v6 on v5

--- a/solution.py
+++ b/solution.py
@@ -39,7 +39,7 @@
            vert, slash, keep, q, ko, vo, kw, vw, kvert, vvert, causal, ebuf_a, ebuf_b, shares, mx, acc0, acc, sc, win, vs,
            s1, r1a, r1b, s2, r2a, r2b, s3, r3a, r3b, full,
            hr, rw, v1, vz,
-           in_sem, slash_s, slash_r, ex_s, ex_r, far_s, far_r, t_s, t_r, h_s, h_r):
+           in_sem, slash_s, slash_r, ex_s, ex_r, far_s, far_r, ready, t_s, t_r, h_s, h_r):
     head = lax.axis_index("head")
     ctx = lax.axis_index("ctx")
     y = ctx // (NL * NH)
@@ -62,7 +62,7 @@
 
     barrier = pltpu.get_barrier_semaphore()
     z_peers = [along(k) for k in (8, 7, -7, 6, -6, 5, -5, 4, -4, 3, -3, 2, -2, 1, -1)]
-    greeted = z_peers + [p for _, p in y_peers + heads] + [after, before]
+    greeted = [along(k) for k in (2, -2, 1, -1)] + [p for _, p in y_peers + heads] + [after, before]
     for p in greeted:
         pl.semaphore_signal(barrier, inc=1, device_id=p, device_id_type=MESH)
 
@@ -146,6 +146,18 @@
 
     send_slash(0)
 
+    def tell(first, distance):
+        for n, k in enumerate((distance, -distance)):
+            pl.semaphore_signal(ready.at[first + n], inc=1, device_id=along(k), device_id_type=MESH)
+
+    def told(first):
+        for n in range(2):
+            pl.semaphore_wait(ready.at[first + n], 1)
+
+    tell(0, 2)
+    told(0)
+    tell(2, 4)
+
     def owner(j, low, count):
         return (vert[0, j] >> low) & (count - 1)
 
@@ -166,6 +178,7 @@
         for c in steps[g, 1]:
             c.start()
     send_slash(1)
+    told(2)
     for g in range(NG):
         arrived(g, 1)
         for jj in range(G):
@@ -412,7 +425,7 @@
             pltpu.VMEM((NY, NV, TILE), F32),
             pltpu.VMEM((NL * NH, NV, TILE), F32),
             dma((8,)), dma((2,)), dma((2,)),
-            dma((NG * 15,)), dma((NG * 15,)), dma((4,)), dma((4,)), dma((18,)), dma((18,)), dma((8,)), dma((8,)),
+            dma((NG * 15,)), dma((NG * 15,)), dma((4,)), dma((4,)), pltpu.SemaphoreType.REGULAR((4,)), dma((18,)), dma((18,)), dma((8,)), dma((8,)),
         ],
         compiler_params=pltpu.CompilerParams(
             collective_id=0, has_side_effects=True, vmem_limit_bytes=56 << 20

time: 67.2 us -> 64.1 us (0.954)
  the two profiles are of different devices: /device:TPU:6 before, /device:TPU:32 now
where the time goes in v6:
time: 64.1 us; the launch traced here: 64 us
  Pallas kernels  61.8 us (96%)
  local copies, waits for them, and re-layouts  1.57 us (2%)
    pallas_call x1, Pallas kernels, local(): pl.pallas_call(kernel, out_shape=(pltpu.VMEM(queries.shape, BF16), pltpu....  61.8 us

profile of v6, /device:TPU:32, one launch (start us, length us, event | category | flops | bytes accessed | tf_op | source)
XLA Modules:
  0.0 64.0 jit_solution(17973285403210063995)
XLA Ops:
  0.6 61.8 %shard_map.85 = (bf16[1024,512]{1,0:T(8,128)(2,1)S(1)}, f32[2,8,128]{2,1,0:T(8,128)S(1)}) custom-call(s32[1,8]{1,0:T(1,128)} %vert_hbm.1, s32[1,2]{1,0:T(1,128)} %slash_hbm.1, s32[1,8]{1,0:T(1,128)} %keep_hbm.1, bf16[1024,512]{1,0:T(8,128)(2,1)} %q_hbm.1, bf16[8,128,128]{2,1,0:T(8,128)(2,1)} %bitcast.4, bf16[8,128,128]{2,1,0:T(8,128)(2,1)} %bitcast.5), custom_call_target="tpu_custom_call" | custom-call | tf_op jit(solution)/shard_map/pallas_call | solution.py:392
  62.4 1.0 %copy.10 = bf16[1024,512]{1,0:T(8,128)(2,1)} copy(bf16[1024,512]{1,0:T(8,128)(2,1)S(1)} %get-tuple-element.9) | data formatting | bytes 2097152
  63.4 0.6 fusion

commit v7 on v6

--- a/solution.py
+++ b/solution.py
@@ -39,7 +39,7 @@
            vert, slash, keep, q, ko, vo, kw, vw, kvert, vvert, causal, ebuf_a, ebuf_b, shares, mx, acc0, acc, sc, win, vs,
            s1, r1a, r1b, s2, r2a, r2b, s3, r3a, r3b, full,
            hr, rw, v1, vz,
-           in_sem, slash_s, slash_r, ex_s, ex_r, far_s, far_r, ready, t_s, t_r, h_s, h_r):
+           in_sem, slash_s, slash_r, ex_s, ex_r, far_s, far_r, last_s, last_r, ready, t_s, t_r, h_s, h_r):
     head = lax.axis_index("head")
     ctx = lax.axis_index("ctx")
     y = ctx // (NL * NH)
@@ -207,7 +207,14 @@
     for g in range(NG):
         arrived(g, 3)
         block = pl.ds(4 * mine[g][0], 4)
-        steps[g, 4] = stage(g, 4, peers[g][0], lambda i: full.at[g, block], lambda i: full.at[g, block])
+        if g == 0:
+            steps[g, 4] = stage(g, 4, y_peers, lambda i: full.at[g, block], lambda i: full.at[g, block])
+        else:
+            parts = [block] * 2 + [pl.ds(4 * zl, 2), pl.ds(4 * zl + 2, 2)]
+            steps[g, 4] = [
+                remote(full.at[g, part], full.at[g, part], last_s.at[n], last_r.at[n], along(k))
+                for n, (part, k) in enumerate(zip(parts, (-1, 1, -2, 2)))
+            ]
         for c in steps[g, 4]:
             c.start()
     send_slash(4)
@@ -425,7 +432,7 @@
             pltpu.VMEM((NY, NV, TILE), F32),
             pltpu.VMEM((NL * NH, NV, TILE), F32),
             dma((8,)), dma((2,)), dma((2,)),
-            dma((NG * 15,)), dma((NG * 15,)), dma((4,)), dma((4,)), pltpu.SemaphoreType.REGULAR((4,)), dma((18,)), dma((18,)), dma((8,)), dma((8,)),
+            dma((NG * 15,)), dma((NG * 15,)), dma((4,)), dma((4,)), dma((4,)), dma((4,)), pltpu.SemaphoreType.REGULAR((4,)), dma((18,)), dma((18,)), dma((8,)), dma((8,)),
         ],
         compiler_params=pltpu.CompilerParams(
             collective_id=0, has_side_effects=True, vmem_limit_bytes=56 << 20

time: 64.1 us -> 64.7 us (level)
  no operation moved by 1% of the time
where the time goes in v7:
time: 64.7 us; the launch traced here: 64.5 us
  Pallas kernels  62.3 us (96%)
  local copies, waits for them, and re-layouts  1.57 us (2%)
    pallas_call x1, Pallas kernels, local(): pl.pallas_call(kernel, out_shape=(pltpu.VMEM(queries.shape, BF16), pltpu....  62.3 us

profile of v7, /device:TPU:32, one launch (start us, length us, event | category | flops | bytes accessed | tf_op | source)
XLA Modules:
  0.0 64.5 jit_solution(4876246926507647927)
XLA Ops:
  0.6 62.3 %shard_map.85 = (bf16[1024,512]{1,0:T(8,128)(2,1)S(1)}, f32[2,8,128]{2,1,0:T(8,128)S(1)}) custom-call(s32[1,8]{1,0:T(1,128)} %vert_hbm.1, s32[1,2]{1,0:T(1,128)} %slash_hbm.1, s32[1,8]{1,0:T(1,128)} %keep_hbm.1, bf16[1024,512]{1,0:T(8,128)(2,1)} %q_hbm.1, bf16[8,128,128]{2,1,0:T(8,128)(2,1)} %bitcast.4, bf16[8,128,128]{2,1,0:T(8,128)(2,1)} %bitcast.5), custom_call_target="tpu_custom_call" | custom-call | tf_op jit(solution)/shard_map/pallas_call | solution.py:399
  63.0 1.0 %copy.10 = bf16[1024,512]{1,0:T(8,128)(2,1)} copy(bf16[1024,512]{1,0:T(8,128)(2,1)S(1)} %get-tuple-element.9) | data formatting | bytes 2097152
  63.9 0.6 fusion
